TPU v7x, 512 devices: a whole 4x4x16 slice. The times are simulated.
512 devices in a mesh: paths: 8 (over y, core), tm: 64 (over z, x).
Axes of the slice: x: 4, y: 4, z: 16, core: 2. Of those that a mesh axis runs over, the one named last changes fastest.
Arguments:
- independent_disturbances: bfloat16 [4096, 32, 1024], P('tm', 'paths'), may hold values from -6 to 6
- starting_driver_values: float32 [32, 1024], P('paths'), may hold values from -6 to 6
- correlation_mixer: bfloat16 [1024, 1024], P('paths'), may hold values from -0.1875 to 0.1875
- log_persistence: float32 [1024], replicated, may hold values from -0.034 to 0
- regime_multiplier: float32 [4096], P('tm'), may hold values from 0.5 to 1
- payoff_per_unit_table: bfloat16 [1024, 128], replicated, may hold values from -0.1875 to 0.1875
- short_yield_coefficients: bfloat16 [1024], replicated, may hold values from -0.1875 to 0.1875
Outputs:
- values: float32 [32, 128], P('paths')
All inputs are finite; a program needn't handle non-finite values.
Results may differ from a plain program's by a relative error of at most 0.0004.
Values may be sent and summed in bfloat16 or wider, within the bound.
A program may use at most 64 MiB of HBM per device.

v0:
```python
import jax
import jax.numpy as jnp
from jax import lax
from jax.sharding import Mesh
from jax.sharding import PartitionSpec as P

TM = ("tm_0", "tm_1")


def filled_with(shard, identity):
    return jax.tree.map(
        lambda a, e: jnp.broadcast_to(jnp.asarray(e, a.dtype), a.shape), shard, identity
    )


def all_in_one(shard, axis):
    leaves = jax.tree.leaves(shard)
    sequence = sorted(range(len(leaves)), key=lambda k: -leaves[k].size)
    width = (1, *leaves[sequence[0]].shape)[-1]
    lines = [
        jnp.pad(leaves[k].reshape(-1), (0, -leaves[k].size % width)).reshape(-1, width)
        for k in sequence
    ]
    both, at, found = (lax.all_gather(jnp.concatenate(lines), axis), 0, {})
    for k, line in zip(sequence, lines):
        piece = both[:, at : at + len(line)].reshape(len(both), -1)
        found[k] = piece[:, : leaves[k].size].reshape(-1, *leaves[k].shape)
        at += len(line)
    numbers = iter(range(len(leaves)))
    return jax.tree.map(lambda _: found[next(numbers)], shard)


def carried_in(shard, axes, combine, identity):
    before = start = filled_with(shard, identity)
    running = shard
    for axis in reversed(axes):
        peers, here = (lax.axis_size(axis), lax.axis_index(axis))
        pieces = all_in_one(running, axis)
        inside, running = (start, start)
        for k in range(peers):
            passed = k < here
            running = combine(running, jax.tree.map(lambda part: part[k], pieces))
            inside = jax.tree.map(lambda new, old: jnp.where(passed, new, old), running, inside)
        before = combine(inside, before)
    return before


def copy_for_each(shard, axis):
    copies = jnp.broadcast_to(shard, (lax.axis_size(axis), *shard.shape))
    return lax.all_to_all(copies, axis, split_axis=0, concat_axis=0, tiled=True)


def combined_pairwise(pieces, combine):
    while len(jax.tree.leaves(pieces)[0]) > 1:
        pieces = jax.vmap(combine)(*(pieces[side::2] for side in (0, 1)))
    return pieces[0]


def prefix(shard, axis, combine, identity):
    peers, here = (lax.axis_size(axis), lax.axis_index(axis))
    passed = jnp.arange(peers) < here

    def kept(part, zero, own):
        part = jnp.where(
            passed.reshape(-1, *(1 for _ in own.shape)), part, jnp.asarray(zero, own.dtype)
        )
        return part

    pieces = copy_for_each(shard, axis)
    return combined_pairwise(kept(pieces, identity, shard), combine)


def of_everyone(shard, axis):
    return copy_for_each(shard, axis).sum(axis=0)


def local(
    independent_disturbances,
    starting_driver_values,
    correlation_mixer,
    log_persistence,
    regime_multiplier,
    payoff_per_unit_table,
    short_yield_coefficients,
):
    slab_days, group_paths, driver_value_history = independent_disturbances.shape
    where_now = lax.axis_index(TM)
    correlated_disturbances = jnp.einsum(
        "spf,fg->spg",
        independent_disturbances,
        lax.all_gather(correlation_mixer, "paths", axis=0, tiled=True),
        preferred_element_type=jnp.float32,
    )
    persistence_multiplier = jnp.exp(log_persistence)
    vol = jnp.sqrt(-jnp.expm1(2.0 * log_persistence))
    leading_element = jnp.where(
        where_now == 0, starting_driver_values, jnp.zeros_like(starting_driver_values)
    )

    def propagate_one_day(carry, operand_tensors):
        state, decay = carry
        random_normal_sample, regime_multiplier_today = operand_tensors
        driver_value_now = persistence_multiplier * regime_multiplier_today
        state = driver_value_now * state + vol * random_normal_sample
        decay = decay * driver_value_now
        return ((state, decay), (state, decay))

    (state, decay), (local_states, local_decays) = lax.scan(
        propagate_one_day,
        (leading_element, jnp.ones((driver_value_history,), jnp.float32)),
        (correlated_disturbances, regime_multiplier),
    )

    def chain(earlier, later):
        return (earlier[0] * later[0], later[0][None, :] * earlier[1] + later[1])

    identity = (
        jnp.ones((driver_value_history,), jnp.float32),
        jnp.zeros((group_paths, driver_value_history), jnp.float32),
    )
    carried = carried_in((decay, state), TM, chain, identity)
    driver_trajectory = local_states + local_decays[:, None, :] * carried[1][None, :, :]
    scenario = driver_trajectory.astype(jnp.bfloat16)
    horizon_days = slab_days * lax.axis_size(TM)
    cash = jnp.einsum(
        "tpf,fk->tpk", scenario, payoff_per_unit_table, preferred_element_type=jnp.float32
    )
    rate = 0.03 + 0.3 * jnp.einsum(
        "tpf,f->tp", scenario, short_yield_coefficients, preferred_element_type=jnp.float32
    )
    running = jnp.cumsum(rate, axis=0)

    def added(earlier, later):
        return earlier + later

    before = prefix(running[-1], TM, added, jnp.zeros((group_paths,), jnp.float32))
    discount = jnp.exp(-(1.0 / 256.0) * (before[None, :] + running))
    partial_sum = jnp.sum(discount[:, :, None] * cash, axis=0) / horizon_days
    return of_everyone(partial_sum, TM)


def solution(mesh):
    split = Mesh(mesh.devices.reshape(mesh.shape["paths"], 16, 4), ("paths", "tm_0", "tm_1"))
    placed = (P(TM, "paths", None), P("paths", None), P("paths", None), P(), P(TM), P(), P())
    return jax.shard_map(
        local, mesh=split, in_specs=placed, out_specs=P("paths", None), check_vma=False
    )
```

profile of v0, /device:TPU:24, one launch (start us, length us, event | category | flops | bytes accessed | tf_op | source)
XLA Modules:
  0.0 236.0 jit_solution(2021905275992335647)
XLA Ops:
  6.5 0.7 all-gather.6.cloned.1.call-update
  7.3 0.7 reshape.283
  8.0 0.7 negate_sqrt_fusion
  8.7 0.7 broadcast_select_fusion.1
  9.5 36.1 %all-gather.6.cloned.1.call-done = bf16[1024,1024]{1,0:T(8,128)(2,1)} async-done(((bf16[128,1024]{1,0:T(8,128)(2,1)}), bf16[1024,1024]{1,0:T(8,128)(2,1)}) %all-gather.6.cloned.1.call-update) | async-done | bytes 2097168 | tf_op jit(solution)/shard_map/all_gather | solution.py:91
  45.6 2.5 %fusion.2 = f32[64,4,1024]{2,0,1:T(8,128)S(1)} fusion(bf16[1024,1024]{1,0:T(8,128)(2,1)} %all-gather.6.cloned.1.call-done, bf16[64,4,1024]{2,1,0:T(4,128)(2,1)} %param.9), kind=kOutput, calls=%fused_computation.7 | convolution fusion | flops 536870912 | bytes 3670016 | tf_op jit(solution)/shard_map/spf,fg->spg/dot_general | solution.py:88
  48.1 85.9 %while.17 = (s32[]{:T(128)}, f32[4,1024]{1,0:T(4,128)S(1)}, f32[1024]{0:T(1024)S(1)}, f32[64,4,1024]{2,1,0:T(4,128)S(1)}, f32[64,1024]{1,0:T(8,128)S(1)}, /*inde...) while((s32[]{:T(128)}, f32[4,1024]{1,0:T(4,128)S(1)}, ...), condition=%wide.region_1.2_spmd.clone, body=%wide.region_0.1_spmd.clone.sunk | while | flops 15363 | bytes 131219 | solution.py:108
  49.5 0.6 dynamic_slice.14
  52.1 0.6 dynamic_slice.14
  53.5 0.6 dynamic_slice.14
  54.8 0.6 dynamic_slice.14
  56.2 0.6 dynamic_slice.14
  58.9 0.6 dynamic_slice.14
  61.5 0.6 dynamic_slice.14
  62.9 0.6 dynamic_slice.14
  65.6 0.6 dynamic_slice.14
  68.3 0.6 dynamic_slice.14
  69.6 0.6 dynamic_slice.14
  70.9 0.6 dynamic_slice.14
  72.3 0.6 dynamic_slice.14
  75.0 0.6 dynamic_slice.14
  77.7 0.6 dynamic_slice.14
  79.0 0.6 dynamic_slice.14
  80.3 0.6 dynamic_slice.14
  81.7 0.6 dynamic_slice.14
  134.1 12.3 %all-gather.2 = f32[4,5,1024]{2,1,0:T(8,128)S(1)} all-gather(f32[1,5,1024]{2,1,0:T(8,128)S(1)} %maximum_bitcast_fusion), channel_id=2, replica_groups=mesh['paths'=8,'tm_0'=16,'tm_1'=4] {'tm_1'}, dimensions={0}, use_global_device_ids=true | all-gather | bytes 102400 | tf_op jit(solution)/shard_map/all_gather | solution.py:24
  146.5 33.2 %all-gather.3 = f32[16,5,1024]{2,1,0:T(8,128)S(1)} all-gather(f32[1,5,1024]{2,1,0:T(8,128)S(1)} %maximum_bitcast_fusion.1), channel_id=3, replica_groups=mesh['paths'=8,'tm_0'=16,'tm_1'=4] {'tm_0'}, dimensions={0}, use_global_device_ids=true | all-gather | bytes 348160 | tf_op jit(solution)/shard_map/all_gather | solution.py:24
  180.8 0.6 broadcast_in_dim.41
  181.4 11.5 %all-to-all-start = ((f32[64,1,4]{2,1,0:T(1,128)}), f32[64,1,4]{2,1,0:T(1,128)S(1)}, u32[]{:S(2)}, u32[]{:S(2)}) async-start(f32[64,1,4]{2,1,0:T(1,128)} %broadcast_in_dim.41), calls=%async_computation | async-start | bytes 65536 | tf_op jit(solution)/shard_map/all_to_all | solution.py:50
  192.9 14.7 %all-to-all-done = f32[64,1,4]{2,1,0:T(1,128)S(1)} async-done(((f32[64,1,4]{2,1,0:T(1,128)}), f32[64,1,4]{2,1,0:T(1,128)S(1)}, u32[]{:S(2)}, u32[]{:S(2)}) %all-to-all-start) | async-done | bytes 1056 | tf_op jit(solution)/shard_map/all_to_all | solution.py:50
  208.4 20.1 %all_to_all.14 = f32[64,4,128]{2,1,0:T(4,128)S(1)} all-to-all(f32[64,4,128]{2,1,0:T(4,128)S(1)} %broadcast_in_dim.43), channel_id=1, replica_groups=mesh['paths'=8,'tm_0'=16,'tm_1'=4] {'tm_0','tm_1'}, dimensions={0} | all-to-all | bytes 262144 | tf_op jit(solution)/shard_map/all_to_all | solution.py:50
  228.5 0.7 reduce_sum.19
  (346 shorter events, 74.7 us)
Async XLA Ops:
  6.5 201.5 %copy-start = (bf16[1024,128]{1,0:T(8,128)(2,1)S(1)}, bf16[1024,128]{1,0:T(8,128)(2,1)}, u32[]{:S(2)}) copy-start(bf16[1024,128]{1,0:T(8,128)(2,1)} %param.14) | copy-start | bytes 786436
  6.5 41.6 %copy-start.1 = (f32[64]{0:T(128)S(1)}, f32[64]{0:T(128)}, u32[]{:S(2)}) copy-start(f32[64]{0:T(128)} %param.13) | copy-start | bytes 772
  6.5 39.1 %all-gather.6.cloned.1.call-start = ((), (), s32[]{:S(2)}) async-start(), calls=%async_computation.2 | async-start | bytes 2359296 | tf_op jit(solution)/shard_map/all_gather | solution.py:91
  181.4 26.2 %all-to-all-start = ((f32[64,1,4]{2,1,0:T(1,128)}), f32[64,1,4]{2,1,0:T(1,128)S(1)}, u32[]{:S(2)}, u32[]{:S(2)}) async-start(f32[64,1,4]{2,1,0:T(1,128)} %broadcast_in_dim.41), calls=%async_computation | async-start | bytes 65536 | tf_op jit(solution)/shard_map/all_to_all | solution.py:50
Sparse Core Ops, SparseCore 0:
  9.5 36.0 all-gather.5
where the time goes:
time: 237 us; the launch traced here: 236 us
  blocking collectives  65.6 us (28%)
  waiting for transfers between devices  51.6 us (22%)
  local copies, waits for them, and re-layouts  47.2 us (20%)
  other arithmetic  40.6 us (17%)
  between operations  13.6 us (6%)
  starting transfers between devices  11.5 us (5%)
  matrix products  3.14 us (1%)
  loops' own time  2.69 us (1%)
    all_gather x2, blocking collectives, all_in_one(): both, at, found = (lax.all_gather(jnp.concatenate(lines), axis), 0, {})  45.6 us
    dynamic_slice x128, local copies, waits for them, and re-layouts, local(): lax.scan(propagate_one_day, (leading_element, jnp.ones((driver_value_hist...  38.5 us
    all_gather x1, waiting for transfers between devices, local(): lax.all_gather(correlation_mixer, 'paths', axis=0, tiled=True)  36.1 us
    mul x64, other arithmetic, propagate_one_day(): decay = decay * driver_value_now  36 us
    all_to_all x1, blocking collectives, copy_for_each(): return lax.all_to_all(copies, axis, split_axis=0, concat_axis=0, tiled=True)  20.1 us
    all_to_all x1, waiting for transfers between devices, copy_for_each(): return lax.all_to_all(copies, axis, split_axis=0, concat_axis=0, tiled=True)  14.7 us
    all_to_all x1, starting transfers between devices, copy_for_each(): return lax.all_to_all(copies, axis, split_axis=0, concat_axis=0, tiled=True)  11.5 us
    dynamic_update_slice x64, local copies, waits for them, and re-layouts, local(): lax.scan(propagate_one_day, (leading_element, jnp.ones((driver_value_hist...  7.04 us
  transfers between devices with their start and end apart: 2, of which 2 were waited for; matrix products, arithmetic and copies ran while one was open for 1% of the time, Pallas kernels for 0%

commit v1 on v0

v1 whole, which is shorter than its diff:
```python
import functools

import jax
import jax.numpy as jnp
from jax import lax
from jax.experimental import pallas as pl
from jax.experimental.pallas import tpu as pltpu
from jax.sharding import Mesh
from jax.sharding import PartitionSpec as P

MESH_ID = pl.DeviceIdType.MESH
NY, NC, NZ, NX = 4, 2, 16, 4
DAYS, PATHS, F, K = 64, 4, 1024, 128
BLOCK = DAYS * NX
LANES = 128
FAR_FIRST = (8, 7, 9, 6, 10, 5, 11, 4, 12, 3, 13, 2, 14, 1, 15)
f32, bf16 = jnp.float32, jnp.bfloat16


def columns(k):
    return pl.ds(pl.multiple_of(k * LANES, LANES), LANES)


def expm1(v):
    total = jnp.ones_like(v)
    for n in range(10, 1, -1):
        total = 1.0 + total * v * (1.0 / n)
    return v * total


def remote(src, dst, send, recv, **where):
    return pltpu.make_async_remote_copy(
        src_ref=src, dst_ref=dst, send_sem=send, recv_sem=recv, device_id=where, device_id_type=MESH_ID
    )


def kernel(
    e_in, s0_in, m_in, lp_in, lpd_in, reg_in, pay_in, sc_in, out,
    ev, es, er, mb, bm, acc, dd, scen, res, rw, rb, lpv, lpd, s0v, regv, scv,
    dk, dx, dt, uu, vv, lrs, lrr, ebs, ebr, cbs, fs, fr, gs, gr,
    ld, msend, mrecv, esend, erecv, rsend, rrecv, lsend, lrecv, bsend, brecv, fsend, frecv, gsend, grecv,
):
    y, c, z, x = (lax.axis_index(a) for a in ("y", "c", "z", "x"))
    yp, ym, y2 = lax.rem(y + 1, NY), lax.rem(y + NY - 1, NY), lax.rem(y + 2, NY)
    mate = 1 - c

    def shard(yy, cc, half):
        return mb.at[pl.ds(pl.multiple_of((yy * 2 + cc) * 128 + half * 64, 64), 64), :]

    loads = [
        pltpu.make_async_copy(e_in, ev, ld.at[0]),
        pltpu.make_async_copy(reg_in, regv, ld.at[1]),
        pltpu.make_async_copy(lp_in, lpv, ld.at[2]),
        pltpu.make_async_copy(lpd_in, lpd, ld.at[3]),
        pltpu.make_async_copy(s0_in, s0v, ld.at[4]),
        pltpu.make_async_copy(sc_in, scv, ld.at[5]),
        pltpu.make_async_copy(pay_in, bm.at[:, pl.ds(0, K)], ld.at[6]),
        pltpu.make_async_copy(m_in, mb.at[pl.ds(pl.multiple_of((y * 2 + c) * 128, 128), 128), :], ld.at[7]),
    ]
    for copy in loads:
        copy.start()

    barrier = pltpu.get_barrier_semaphore()
    peers = [{"c": mate}, {"y": yp}, {"y": ym}]
    peers += [{"x": lax.rem(x + k, NX)} for k in range(1, NX)]
    for peer in peers:
        pl.semaphore_signal(barrier, inc=1, device_id=peer, device_id_type=MESH_ID)

    @pl.loop(1, NZ)
    def _(k):
        pl.semaphore_signal(barrier, inc=1, device_id={"z": lax.rem(z + k, NZ)}, device_id_type=MESH_ID)

    loads[0].wait()
    row = lax.broadcasted_iota(jnp.int32, (256, 256), 0)
    col = lax.broadcasted_iota(jnp.int32, (256, 256), 1)
    source = (((row & 7) * 8 + ((row >> 3) & 7)) << 2) + (row >> 6)
    order = (col == source).astype(f32).astype(bf16)
    for k in range(4):
        cols = pl.ds(k * 256, 256)
        flat = ev[:, :, cols].reshape(DAYS * PATHS, 256)
        moved = jnp.dot(order, flat, preferred_element_type=f32).astype(bf16)
        for p in range(PATHS):
            es[p, :, cols] = moved[p * DAYS : (p + 1) * DAYS]
    loads[1].wait()
    rw[pl.ds(x, 1)] = jnp.ones((1, 8, LANES), f32)
    rw[pl.ds(x, 1), :, pl.ds(0, DAYS)] = jnp.broadcast_to(regv[...][None], (1, 8, DAYS))

    pl.semaphore_wait(barrier, len(peers) + NZ - 1)

    def m_copy(n, src, dst, **where):
        return remote(src, dst, msend.at[n], mrecv.at[n], **where)

    def own(half):
        return m_in.at[pl.ds(half * 64, 64), :]

    up = [m_copy(h, own(h), shard(y, c, h), y=yp) for h in range(2)]
    down = [m_copy(2 + h, own(h), shard(y, c, h), y=ym) for h in range(2)]
    across = m_copy(4, m_in, mb.at[pl.ds(pl.multiple_of((y * 2 + c) * 128, 128), 128), :], c=mate)
    up[0].start()
    down[1].start()
    r_copies, e_copies = [], []
    for k in range(1, NX):
        xx = lax.rem(x + k, NX)
        r_copies.append(remote(rw.at[x], rw.at[x], rsend.at[k - 1], rrecv.at[x], x=xx))
        e_copies.append(remote(es.at[xx], er.at[x], esend.at[k - 1], erecv.at[x], x=xx))
    for copy in r_copies:
        copy.start()
    across.start()
    up[1].start()
    down[0].start()
    for copy in e_copies:
        copy.start()
    e_own = pltpu.make_async_copy(es.at[x], er.at[x], ld.at[8])
    e_own.start()
    for copy in loads[2:]:
        copy.wait()

    for k in range(F // LANES):
        block = jnp.broadcast_to(scv[:, k * LANES : (k + 1) * LANES].astype(f32), (LANES, LANES))
        bm[pl.ds(k * LANES, LANES), pl.ds(K, LANES)] = block.T.astype(bf16)

    def r_wait(k):
        xx = lax.rem(x + k, NX)
        remote(rw.at[x], rw.at[xx], rsend.at[k - 1], rrecv.at[xx], x=xx).wait_recv()

    for k in range(1, NX):
        r_wait(k)
    rows = lax.broadcasted_iota(jnp.int32, (DAYS, LANES), 0)
    lanes = lax.broadcasted_iota(jnp.int32, (DAYS, LANES), 1)
    pick = lanes == (rows & 7) * 8 + (rows >> 3)
    logs = jnp.zeros((8, LANES), f32)
    for j in range(NX):
        logs = logs + jnp.log(rw[j])
        spread = jnp.where(pick, jnp.broadcast_to(rw[j, 0:1], (DAYS, LANES)), 0.0)
        rb[pl.ds(j * DAYS, DAYS), :] = jnp.broadcast_to(jnp.sum(spread, axis=1, keepdims=True), (DAYS, LANES))
    lrs[...] = jnp.broadcast_to(jnp.sum(logs, axis=1, keepdims=True), (8, LANES))

    def later(k, copy):
        @pl.when(z + k < NZ)
        def _():
            copy(k)

    def lr_copy(k):
        return remote(lrs, lrr.at[z], lsend.at[k], lrecv.at[z], z=lax.rem(z + k, NZ))

    def eb_copy(k):
        return remote(ebs, ebr.at[z], bsend.at[k], brecv.at[z], z=lax.rem(z + k, NZ))

    for k in FAR_FIRST:
        later(k, lambda k: lr_copy(k).start())

    sub = lax.broadcasted_iota(jnp.int32, (8, LANES), 0)

    @pl.loop(0, F // LANES)
    def _(k):
        cols = columns(k)
        keep = jnp.broadcast_to(jnp.exp(lpv[:, cols]), (8, LANES))
        before = jnp.ones((8, LANES), f32)
        for j in range(NX):
            decay = None
            for i in range(8):
                r = pl.ds(j * DAYS + i * 8, 8)
                today = keep * rb[r, :]
                decay = today if i == 0 else decay * today
                dd[r, cols] = decay
            for n, shift in enumerate((1, 2, 4)):
                dk[n, j, :, cols] = jnp.where(sub >= shift, decay, 0.0)
                decay = jnp.where(sub >= shift, decay * pltpu.roll(decay, shift, 0), decay)
            first = jnp.where(sub >= 1, pltpu.roll(decay, 1, 0), 1.0)
            total = jnp.broadcast_to(decay[7:8], (8, LANES))
            dx[j, :, cols] = first
            dt[j, :, cols] = total
            vv[j, :, cols] = first * before
            before = before * total

    def hop(n, yy, half):
        return remote(shard(yy, c, half), shard(yy, c, half), msend.at[n], mrecv.at[n], y=yp)

    def relay(n, yy, half):
        return m_copy(7 + n, shard(yy, c, half), shard(yy, c, half), c=mate)

    def relayed(n, yy, half):
        remote(shard(yy, mate, half), shard(yy, mate, half), msend.at[7 + n], mrecv.at[7 + n], c=mate).wait_recv()

    relays = [relay(0, ym, 0), relay(1, yp, 1), relay(2, ym, 1), relay(3, yp, 0), relay(4, y2, 0), relay(5, y2, 1)]
    up2 = m_copy(5, shard(ym, c, 0), shard(ym, c, 0), y=yp)
    down2 = m_copy(6, shard(yp, c, 1), shard(yp, c, 1), y=ym)

    def product(yy, first):
        at = pl.ds(pl.multiple_of(yy * 256, 256), 256)
        left = jnp.concatenate([er[j, :, at] for j in range(NX)], axis=0)
        for k in range(4):
            cols = pl.ds(k * 256, 256)
            term = jnp.dot(left, mb[at, cols], preferred_element_type=f32)
            acc[:, cols] = term if first else acc[:, cols] + term

    hop(0, ym, 0).wait_recv()
    up2.start()
    relays[0].start()
    hop(3, yp, 1).wait_recv()
    down2.start()
    relays[1].start()
    e_own.wait()
    for k in range(1, NX):
        xx = lax.rem(x + k, NX)
        remote(es.at[xx], er.at[xx], esend.at[k - 1], erecv.at[xx], x=xx).wait_recv()
    remote(m_in, mb.at[pl.ds(pl.multiple_of((y * 2 + mate) * 128, 128), 128), :], msend.at[4], mrecv.at[4], c=mate).wait_recv()
    product(y, True)
    hop(1, ym, 1).wait_recv()
    relays[2].start()
    hop(2, yp, 0).wait_recv()
    relays[3].start()
    relayed(0, ym, 0)
    relayed(2, ym, 1)
    product(ym, False)
    hop(5, y2, 0).wait_recv()
    relays[4].start()
    hop(6, y2, 1).wait_recv()
    relays[5].start()
    relayed(1, yp, 1)
    relayed(3, yp, 0)
    product(yp, False)
    relayed(4, y2, 0)
    relayed(5, y2, 1)
    product(y2, False)

    @pl.loop(0, F // LANES)
    def _(k):
        cols = columns(k)
        log_keep = lpv[:, cols]
        keep = jnp.broadcast_to(jnp.exp(log_keep), (8, LANES))
        double = 2.0 * log_keep
        vol = jnp.broadcast_to(jnp.sqrt(-expm1(double)), (8, LANES))
        carried = jnp.zeros((8, LANES), f32)
        for j in range(NX):
            state = None
            for i in range(8):
                r = pl.ds(j * DAYS + i * 8, 8)
                shock = vol * acc[r, cols]
                state = shock if i == 0 else (keep * rb[r, :]) * state + shock
                acc[r, cols] = state
            for n, shift in enumerate((1, 2, 4)):
                state = state + dk[n, j, :, cols] * pltpu.roll(state, shift, 0)
            first = jnp.where(sub >= 1, pltpu.roll(state, 1, 0), 0.0)
            uu[j, :, cols] = first + dx[j, :, cols] * carried
            carried = dt[j, :, cols] * carried + jnp.broadcast_to(state[7:8], (8, LANES))
        ebs[pl.ds(k, 1), :] = carried[0:1]

    for k in FAR_FIRST:
        later(k, lambda k: eb_copy(k).start())

    @pl.loop(0, F // LANES)
    def _(k):
        cols = columns(k)
        paths = lax.broadcasted_iota(jnp.int32, (PATHS, LANES), 0)
        cbs[pl.ds(k, 1), :] = jnp.sum(jnp.where(paths == x, s0v[:, cols], 0.0), axis=0, keepdims=True)
        for j in range(NX):
            u, v = uu[j, :, cols], vv[j, :, cols]
            for i in range(8):
                r = pl.ds(j * DAYS + i * 8, 8)
                decay = dd[r, cols]
                acc[r, cols] = acc[r, cols] + decay * u
                dd[r, cols] = decay * v

    span = float(BLOCK) * lpd[...]

    @pl.loop(0, z)
    def _(u):
        remote(lrs, lrr.at[u], lsend.at[0], lrecv.at[u], z=u).wait_recv()
        lrr[pl.ds(u, 1)] = jnp.exp(span + lrr[u])[None]

    def entered(u, carry):
        remote(ebs, ebr.at[u], bsend.at[0], brecv.at[u], z=u).wait_recv()
        return lrr[u] * carry + ebr[u]

    cbs[...] = lax.fori_loop(0, z, entered, cbs[...])

    @pl.loop(0, F // LANES)
    def _(k):
        cols = columns(k)
        scen[:, cols] = (acc[:, cols] + dd[:, cols] * cbs[pl.ds(k, 1), :]).astype(bf16)

    res[...] = jnp.dot(scen[...], bm[...], preferred_element_type=f32)

    base = jnp.zeros((8, LANES), f32)
    exponent = []
    for j in range(NX):
        run = jnp.zeros((8, LANES), f32)
        sums = []
        for i in range(8):
            run = run + (0.03 + 0.3 * res[pl.ds(j * DAYS + i * 8, 8), pl.ds(K, LANES)])
            sums.append(run)
        total = run
        for shift in (1, 2, 4):
            total = total + jnp.where(sub >= shift, pltpu.roll(total, shift, 0), 0.0)
        start = base + jnp.where(sub >= 1, pltpu.roll(total, 1, 0), 0.0)
        base = base + jnp.broadcast_to(total[7:8], (8, LANES))
        exponent += [(-1.0 / 256.0) * (start + s) for s in sums]
    top = functools.reduce(jnp.maximum, exponent)
    top = jnp.max(top, axis=0, keepdims=True)
    worth = jnp.zeros((8, LANES), f32)
    for n, power in enumerate(exponent):
        worth = worth + jnp.exp(power - top) * res[pl.ds(n * 8, 8), pl.ds(0, K)]
    fs[0:1, :] = jnp.sum(worth, axis=0, keepdims=True)
    fs[1:2, :] = base[0:1]
    fs[2:3, :] = top
    fs[3:4, :] = top
    fr[pl.ds(z, 1)] = fs[...][None]

    def f_copy(k):
        return remote(fs, fr.at[z], fsend.at[k], frecv.at[z], z=lax.rem(z + k, NZ))

    for k in FAR_FIRST:
        f_copy(k).start()
    for k in reversed(FAR_FIRST):
        u = lax.rem(z + k, NZ)
        remote(fs, fr.at[u], fsend.at[k], frecv.at[u], z=u).wait_recv()

    passed = jnp.zeros((1, LANES), f32)
    value = jnp.zeros((1, LANES), f32)
    for u in range(NZ):
        value = value + jnp.exp(fr[u, 2:3] - (1.0 / 256.0) * passed) * fr[u, 0:1]
        passed = passed + fr[u, 1:2]
    gs[...] = jnp.broadcast_to(value * (1.0 / 4096.0), (8, LANES))
    g_copies = []
    for k in range(1, NX):
        xx = lax.rem(x + k, NX)
        g_copies.append(remote(gs, gr.at[x], gsend.at[k - 1], grecv.at[x], x=xx))
        g_copies[-1].start()
    gr[pl.ds(x, 1)] = gs[...][None]

    for copy in (*up, *down, across, up2, down2, *relays, *r_copies, *e_copies):
        copy.wait_send()
    for k in FAR_FIRST:
        later(k, lambda k: lr_copy(k).wait_send())
        later(k, lambda k: eb_copy(k).wait_send())
        f_copy(k).wait_send()
    for k in range(1, NX):
        xx = lax.rem(x + k, NX)
        remote(gs, gr.at[xx], gsend.at[k - 1], grecv.at[xx], x=xx).wait_recv()
    for j in range(NX):
        out[j : j + 1, :] = gr[j, 0:1]
    for copy in g_copies:
        copy.wait_send()


def local(e, s0, m, lp, reg, pay, sc):
    vmem, dma = pltpu.VMEM, pltpu.SemaphoreType.DMA
    return pl.pallas_call(
        kernel,
        out_shape=jax.ShapeDtypeStruct((PATHS, K), f32),
        in_specs=[pl.BlockSpec(memory_space=pl.ANY)] * 8,
        out_specs=pl.BlockSpec(memory_space=pltpu.VMEM),
        scratch_shapes=[
            vmem((DAYS, PATHS, F), bf16),
            vmem((PATHS, DAYS, F), bf16),
            vmem((NX, DAYS, F), bf16),
            vmem((F, F), bf16),
            vmem((F, 2 * K), bf16),
            vmem((BLOCK, F), f32),
            vmem((BLOCK, F), f32),
            vmem((BLOCK, F), bf16),
            vmem((BLOCK, 2 * K), f32),
            vmem((NX, 8, LANES), f32),
            vmem((BLOCK, LANES), f32),
            vmem((1, F), f32),
            vmem((8, LANES), f32),
            vmem((PATHS, F), f32),
            vmem((1, DAYS), f32),
            vmem((1, F), bf16),
            vmem((3, NX, 8, F), f32),
            vmem((NX, 8, F), f32),
            vmem((NX, 8, F), f32),
            vmem((NX, 8, F), f32),
            vmem((NX, 8, F), f32),
            vmem((8, LANES), f32),
            vmem((NZ, 8, LANES), f32),
            vmem((8, LANES), f32),
            vmem((NZ, 8, LANES), f32),
            vmem((8, LANES), f32),
            vmem((4, LANES), f32),
            vmem((NZ, 4, LANES), f32),
            vmem((8, LANES), f32),
            vmem((NX, 8, LANES), f32),
            dma((9,)),
            dma((13,)), dma((13,)),
            dma((NX,)), dma((NX,)),
            dma((NX,)), dma((NX,)),
            dma((NZ,)), dma((NZ,)),
            dma((NZ,)), dma((NZ,)),
            dma((NZ,)), dma((NZ,)),
            dma((NX,)), dma((NX,)),
        ],
        compiler_params=pltpu.CompilerParams(collective_id=0, has_side_effects=True, vmem_limit_bytes=48 << 20),
        name="scenarios",
    )(e, s0, m, lp.reshape(1, F), lp.reshape(8, LANES), reg.reshape(1, DAYS), pay, sc.reshape(1, F))


def solution(mesh):
    split = Mesh(mesh.devices.reshape(NY, NC, NZ, NX), ("y", "c", "z", "x"))
    paths, days = ("y", "c"), ("z", "x")
    placed = (P(days, paths, None), P(paths, None), P(paths, None), P(), P(days), P(), P())
    return jax.shard_map(local, mesh=split, in_specs=placed, out_specs=P(paths, None), check_vma=False)
```

time: 237 us -> 54.6 us (0.23)
  the two profiles are of different devices: /device:TPU:24 before, /device:TPU:1 now
where the time goes in v1:
time: 54.6 us; the launch traced here: 54.3 us
  Pallas kernels  48.7 us (89%)
  local copies, waits for them, and re-layouts  5.57 us (10%)
    pallas_call x1, Pallas kernels, local(): pl.pallas_call(kernel, out_shape=jax.ShapeDtypeStruct((PATHS, K), f32), i...  48.7 us
    unnamed x15, local copies, waits for them, and re-layouts  5.57 us

profile of v1, /device:TPU:1, one launch (start us, length us, event | category | flops | bytes accessed | tf_op | source)
XLA Modules:
  0.0 54.3 jit_solution(13279719041961101917)
XLA Ops:
  0.0 0.0 copy-start.6
  0.0 0.0 copy-start.4
  0.0 0.7 %copy-done.6 = bf16[1024]{0:T(1024)(128)(2,1)S(1)} copy-done((bf16[1024]{0:T(1024)(128)(2,1)S(1)}, bf16[1024]{0:T(1024)(128)(2,1)}, u32[]{:S(2)}) %copy-start.6) | copy-done | bytes 2072
  0.7 0.0 copy-start.5
  0.7 0.0 copy-done.4
  0.7 0.6 %copy-done.5 = f32[64]{0:T(128)S(1)} copy-done((f32[64]{0:T(128)S(1)}, f32[64]{0:T(128)}, u32[]{:S(2)}) %copy-start.5) | copy-done | bytes 280
  1.3 0.0 copy-start
  1.3 1.0 %copy-done = bf16[64,4,1024]{2,1,0:T(4,128)(2,1)S(1)} copy-done((bf16[64,4,1024]{2,1,0:T(4,128)(2,1)S(1)}, bf16[64,4,1024]{2,1,0:T(4,128)(2,1)}, u32[]{:S(2)}) %copy-start) | copy-done | bytes 524312
  2.4 0.0 copy-start.1
  2.4 0.9 %copy-done.1 = bf16[128,1024]{1,0:T(8,128)(2,1)S(1)} copy-done((bf16[128,1024]{1,0:T(8,128)(2,1)S(1)}, bf16[128,1024]{1,0:T(8,128)(2,1)}, u32[]{:S(2)}) %copy-start.1) | copy-done | bytes 262168
  3.3 0.0 copy-start.2
  3.3 0.9 %copy-done.2 = bf16[1024,128]{1,0:T(8,128)(2,1)S(1)} copy-done((bf16[1024,128]{1,0:T(8,128)(2,1)S(1)}, bf16[1024,128]{1,0:T(8,128)(2,1)}, u32[]{:S(2)}) %copy-start.2) | copy-done | bytes 262168
  4.3 0.0 copy-start.3
  4.3 0.7 %copy-done.3 = f32[4,1024]{1,0:T(4,128)S(1)} copy-done((f32[4,1024]{1,0:T(4,128)S(1)}, f32[4,1024]{1,0:T(4,128)}, u32[]{:S(2)}) %copy-start.3) | copy-done | bytes 16408
  5.0 48.7 %scenarios.1 = f32[4,128]{1,0:T(4,128)S(1)} custom-call(bf16[64,4,1024]{2,1,0:T(4,128)(2,1)S(1)} %copy-done, f32[4,1024]{1,0:T(4,128)S(1)} %copy-done.3, bf16[128,1024]{1,0:T(8,128)(2,1)S(1)} %copy-done.1, f32[1,1024]{1,0:T(1,128)S(1)} %bitcast.3, f32[8,128]{1,0:T(8,128)S(1)} %bitcast.4, f32[1,64]{1,0:T(1,128)S(1)} %bitcast.5, ...), custom_call_target="tpu_custom_call" | custom-call | tf_op jit(solution)/shard_map/scenarios/pallas_call | solution.py:349
  53.7 0.6 %copy.9 = f32[4,128]{1,0:T(4,128)} copy(f32[4,128]{1,0:T(4,128)S(1)} %scenarios.1) | data formatting | bytes 4096
  (1 shorter events, 0.0 us)
Async XLA Ops:
  0.0 0.7 %copy-start.6 = (bf16[1024]{0:T(1024)(128)(2,1)S(1)}, bf16[1024]{0:T(1024)(128)(2,1)}, u32[]{:S(2)}) copy-start(bf16[1024]{0:T(1024)(128)(2,1)} %param.13) | copy-start | bytes 6148
  0.0 0.7 %copy-start.4 = (f32[1024]{0:T(1024)S(1)}, f32[1024]{0:T(1024)}, u32[]{:S(2)}) copy-start(f32[1024]{0:T(1024)} %param.10) | copy-start | bytes 12292
  0.7 0.7 %copy-start.5 = (f32[64]{0:T(128)S(1)}, f32[64]{0:T(128)}, u32[]{:S(2)}) copy-start(f32[64]{0:T(128)} %param.11) | copy-start | bytes 772
  1.3 1.0 %copy-start = (bf16[64,4,1024]{2,1,0:T(4,128)(2,1)S(1)}, bf16[64,4,1024]{2,1,0:T(4,128)(2,1)}, u32[]{:S(2)}) copy-start(bf16[64,4,1024]{2,1,0:T(4,128)(2,1)} %e_in.1) | copy-start | bytes 1572868
  2.4 0.9 %copy-start.1 = (bf16[128,1024]{1,0:T(8,128)(2,1)S(1)}, bf16[128,1024]{1,0:T(8,128)(2,1)}, u32[]{:S(2)}) copy-start(bf16[128,1024]{1,0:T(8,128)(2,1)} %m_in.1) | copy-start | bytes 786436
  3.3 0.9 %copy-start.2 = (bf16[1024,128]{1,0:T(8,128)(2,1)S(1)}, bf16[1024,128]{1,0:T(8,128)(2,1)}, u32[]{:S(2)}) copy-start(bf16[1024,128]{1,0:T(8,128)(2,1)} %pay_in.1) | copy-start | bytes 786436
  4.3 0.7 %copy-start.3 = (f32[4,1024]{1,0:T(4,128)S(1)}, f32[4,1024]{1,0:T(4,128)}, u32[]{:S(2)}) copy-start(f32[4,1024]{1,0:T(4,128)} %s0_in.1) | copy-start | bytes 49156

commit v2 on v1

--- a/solution.py
+++ b/solution.py
@@ -38,7 +38,7 @@
     e_in, s0_in, m_in, lp_in, lpd_in, reg_in, pay_in, sc_in, out,
     ev, es, er, mb, bm, acc, dd, scen, res, rw, rb, lpv, lpd, s0v, regv, scv,
     dk, dx, dt, uu, vv, lrs, lrr, ebs, ebr, cbs, fs, fr, gs, gr,
-    ld, msend, mrecv, esend, erecv, rsend, rrecv, lsend, lrecv, bsend, brecv, fsend, frecv, gsend, grecv,
+    ld, msend, mrecv, esend, erecv, rsend, rrecv, lsend, lrecv, bsend, brecv, fsend, frecv, gsend, grecv, met,
 ):
     y, c, z, x = (lax.axis_index(a) for a in ("y", "c", "z", "x"))
     yp, ym, y2 = lax.rem(y + 1, NY), lax.rem(y + NY - 1, NY), lax.rem(y + 2, NY)
@@ -66,9 +66,11 @@
     for peer in peers:
         pl.semaphore_signal(barrier, inc=1, device_id=peer, device_id_type=MESH_ID)
 
-    @pl.loop(1, NZ)
-    def _(k):
-        pl.semaphore_signal(barrier, inc=1, device_id={"z": lax.rem(z + k, NZ)}, device_id_type=MESH_ID)
+    def along_z(semaphore, distance):
+        for k in (distance, NZ - distance):
+            pl.semaphore_signal(semaphore, inc=1, device_id={"z": lax.rem(z + k, NZ)}, device_id_type=MESH_ID)
+
+    along_z(barrier, 1)
 
     loads[0].wait()
     row = lax.broadcasted_iota(jnp.int32, (256, 256), 0)
@@ -85,7 +87,8 @@
     rw[pl.ds(x, 1)] = jnp.ones((1, 8, LANES), f32)
     rw[pl.ds(x, 1), :, pl.ds(0, DAYS)] = jnp.broadcast_to(regv[...][None], (1, 8, DAYS))
 
-    pl.semaphore_wait(barrier, len(peers) + NZ - 1)
+    pl.semaphore_wait(barrier, len(peers) + 2)
+    along_z(met.at[0], 1)
 
     def m_copy(n, src, dst, **where):
         return remote(src, dst, msend.at[n], mrecv.at[n], **where)
@@ -115,8 +118,9 @@
     for copy in loads[2:]:
         copy.wait()
 
+    short = scv[...].astype(f32)
     for k in range(F // LANES):
-        block = jnp.broadcast_to(scv[:, k * LANES : (k + 1) * LANES].astype(f32), (LANES, LANES))
+        block = jnp.broadcast_to(short[k : k + 1], (LANES, LANES))
         bm[pl.ds(k * LANES, LANES), pl.ds(K, LANES)] = block.T.astype(bf16)
 
     def r_wait(k):
@@ -145,9 +149,6 @@
 
     def eb_copy(k):
         return remote(ebs, ebr.at[z], bsend.at[k], brecv.at[z], z=lax.rem(z + k, NZ))
-
-    for k in FAR_FIRST:
-        later(k, lambda k: lr_copy(k).start())
 
     sub = lax.broadcasted_iota(jnp.int32, (8, LANES), 0)
 
@@ -206,6 +207,8 @@
         remote(es.at[xx], er.at[xx], esend.at[k - 1], erecv.at[xx], x=xx).wait_recv()
     remote(m_in, mb.at[pl.ds(pl.multiple_of((y * 2 + mate) * 128, 128), 128), :], msend.at[4], mrecv.at[4], c=mate).wait_recv()
     product(y, True)
+    pl.semaphore_wait(met.at[0], 2)
+    along_z(met.at[1], 2)
     hop(1, ym, 1).wait_recv()
     relays[2].start()
     hop(2, yp, 0).wait_recv()
@@ -213,6 +216,8 @@
     relayed(0, ym, 0)
     relayed(2, ym, 1)
     product(ym, False)
+    pl.semaphore_wait(met.at[1], 2)
+    along_z(met.at[2], 4)
     hop(5, y2, 0).wait_recv()
     relays[4].start()
     hop(6, y2, 1).wait_recv()
@@ -220,6 +225,9 @@
     relayed(1, yp, 1)
     relayed(3, yp, 0)
     product(yp, False)
+    pl.semaphore_wait(met.at[2], 2)
+    for k in FAR_FIRST:
+        later(k, lambda k: lr_copy(k).start())
     relayed(4, y2, 0)
     relayed(5, y2, 1)
     product(y2, False)
@@ -367,7 +375,7 @@
             vmem((8, LANES), f32),
             vmem((PATHS, F), f32),
             vmem((1, DAYS), f32),
-            vmem((1, F), bf16),
+            vmem((8, LANES), bf16),
             vmem((3, NX, 8, F), f32),
             vmem((NX, 8, F), f32),
             vmem((NX, 8, F), f32),
@@ -390,10 +398,11 @@
             dma((NZ,)), dma((NZ,)),
             dma((NZ,)), dma((NZ,)),
             dma((NX,)), dma((NX,)),
+            pltpu.SemaphoreType.REGULAR((3,)),
         ],
-        compiler_params=pltpu.CompilerParams(collective_id=0, has_side_effects=True, vmem_limit_bytes=48 << 20),
+        compiler_params=pltpu.CompilerParams(collective_id=0, has_side_effects=True, vmem_limit_bytes=60 << 20),
         name="scenarios",
-    )(e, s0, m, lp.reshape(1, F), lp.reshape(8, LANES), reg.reshape(1, DAYS), pay, sc.reshape(1, F))
+    )(e, s0, m, lp.reshape(1, F), lp.reshape(8, LANES), reg.reshape(1, DAYS), pay, sc.reshape(8, LANES))
 
 
 def solution(mesh):

time: 54.6 us -> 51.4 us (0.941)
  local copies, waits for them, and re-layouts: 5.57 us -> 1.26 us
  Pallas kernels: 48.7 us -> 49.4 us
    unnamed x15 -> x1, local copies, waits for them, and re-layouts: 5.57 us -> 1.26 us
    pallas_call x1, Pallas kernels: 48.7 us -> 49.4 us  [local(): pl.pallas_call(kernel, out_shape=jax.ShapeDtypeStruct((PATHS, K), f32), i...]
where the time goes in v2:
time: 51.4 us; the launch traced here: 50.7 us
  Pallas kernels  49.4 us (96%)
  local copies, waits for them, and re-layouts  1.26 us (2%)
    pallas_call x1, Pallas kernels, local(): pl.pallas_call(kernel, out_shape=jax.ShapeDtypeStruct((PATHS, K), f32), i...  49.4 us
    unnamed x1, local copies, waits for them, and re-layouts  1.26 us

profile of v2, /device:TPU:1, one launch (start us, length us, event | category | flops | bytes accessed | tf_op | source)
XLA Modules:
  0.0 50.7 jit_solution(17737066527678416400)
XLA Ops:
  0.0 49.4 %scenarios.1 = f32[4,128]{1,0:T(4,128)} custom-call(bf16[64,4,1024]{2,1,0:T(4,128)(2,1)} %e_in.1, f32[4,1024]{1,0:T(4,128)} %s0_in.1, bf16[128,1024]{1,0:T(8,128)(2,1)} %m_in.1, f32[1,1024]{1,0:T(1,128)} %bitcast.4, f32[8,128]{1,0:T(8,128)} %bitcast.5, f32[1,64]{1,0:T(1,128)} %bitcast.7, bf16[1024,128]{1,0:T(8,128)(2,1)} %pay_in.1, bf16[8,128]{1,0:T(8,128)(2,1)} %bitcast.6), custom_call_target="tpu_custom_call" | custom-call | tf_op jit(solution)/shard_map/scenarios/pallas_call | solution.py:357
  49.5 1.3 %copy.9 = f32[4,128]{1,0:T(4,128)} copy(f32[4,128]{1,0:T(4,128)} %scenarios.1) | data formatting | bytes 4096

commit v3 on v2

--- a/solution.py
+++ b/solution.py
@@ -12,6 +12,7 @@
 NY, NC, NZ, NX = 4, 2, 16, 4
 DAYS, PATHS, F, K = 64, 4, 1024, 128
 BLOCK = DAYS * NX
+PIECE = 32
 LANES = 128
 FAR_FIRST = (8, 7, 9, 6, 10, 5, 11, 4, 12, 3, 13, 2, 14, 1, 15)
 f32, bf16 = jnp.float32, jnp.bfloat16
@@ -37,15 +38,15 @@
 def kernel(
     e_in, s0_in, m_in, lp_in, lpd_in, reg_in, pay_in, sc_in, out,
     ev, es, er, mb, bm, acc, dd, scen, res, rw, rb, lpv, lpd, s0v, regv, scv,
-    dk, dx, dt, uu, vv, lrs, lrr, ebs, ebr, cbs, fs, fr, gs, gr,
-    ld, msend, mrecv, esend, erecv, rsend, rrecv, lsend, lrecv, bsend, brecv, fsend, frecv, gsend, grecv, met,
+    dk, dx, dt, uu, vv, lrs, lrr, ebs, ebr, cbs, fs, fr,
+    ld, msend, mrecv, esend, erecv, rsend, rrecv, lsend, lrecv, bsend, brecv, fsend, frecv, met,
 ):
     y, c, z, x = (lax.axis_index(a) for a in ("y", "c", "z", "x"))
     yp, ym, y2 = lax.rem(y + 1, NY), lax.rem(y + NY - 1, NY), lax.rem(y + 2, NY)
     mate = 1 - c
 
-    def shard(yy, cc, half):
-        return mb.at[pl.ds(pl.multiple_of((yy * 2 + cc) * 128 + half * 64, 64), 64), :]
+    def shard(yy, cc, piece):
+        return mb.at[pl.ds(pl.multiple_of((yy * 2 + cc) * 128 + piece * PIECE, PIECE), PIECE), :]
 
     loads = [
         pltpu.make_async_copy(e_in, ev, ld.at[0]),
@@ -93,28 +94,32 @@
     def m_copy(n, src, dst, **where):
         return remote(src, dst, msend.at[n], mrecv.at[n], **where)
 
-    def own(half):
-        return m_in.at[pl.ds(half * 64, 64), :]
-
-    up = [m_copy(h, own(h), shard(y, c, h), y=yp) for h in range(2)]
-    down = [m_copy(2 + h, own(h), shard(y, c, h), y=ym) for h in range(2)]
-    across = m_copy(4, m_in, mb.at[pl.ds(pl.multiple_of((y * 2 + c) * 128, 128), 128), :], c=mate)
-    up[0].start()
-    down[1].start()
+    def own(piece):
+        return m_in.at[pl.ds(piece * PIECE, PIECE), :]
+
+    up = [m_copy(n, own(n), shard(y, c, n), y=yp) for n in range(4)]
+    down = [m_copy(4 + n, own(n), shard(y, c, n), y=ym) for n in range(4)]
+    across = m_copy(8, m_in, mb.at[pl.ds(pl.multiple_of((y * 2 + c) * 128, 128), 128), :], c=mate)
     r_copies, e_copies = [], []
     for k in range(1, NX):
         xx = lax.rem(x + k, NX)
         r_copies.append(remote(rw.at[x], rw.at[x], rsend.at[k - 1], rrecv.at[x], x=xx))
         e_copies.append(remote(es.at[xx], er.at[x], esend.at[k - 1], erecv.at[x], x=xx))
+    up[0].start()
+    down[3].start()
     for copy in r_copies:
         copy.start()
-    across.start()
-    up[1].start()
-    down[0].start()
     for copy in e_copies:
         copy.start()
+    for n in (1, 2, 3):
+        up[n].start()
+        down[3 - n].start()
+    across.start()
     e_own = pltpu.make_async_copy(es.at[x], er.at[x], ld.at[8])
     e_own.start()
+
+    pl.semaphore_wait(met.at[0], 2)
+    along_z(met.at[1], 2)
     for copy in loads[2:]:
         copy.wait()
 
@@ -122,6 +127,27 @@
     for k in range(F // LANES):
         block = jnp.broadcast_to(short[k : k + 1], (LANES, LANES))
         bm[pl.ds(k * LANES, LANES), pl.ds(K, LANES)] = block.T.astype(bf16)
+
+    def hop(n, yy, piece):
+        remote(shard(yy, c, piece), shard(yy, c, piece), msend.at[n], mrecv.at[n], y=yp).wait_recv()
+
+    def relay(n, yy, piece):
+        relays.append(m_copy(13 + n, shard(yy, c, piece), shard(yy, c, piece), c=mate))
+        relays[-1].start()
+
+    def relayed(n, yy, piece):
+        remote(shard(yy, mate, piece), shard(yy, mate, piece), msend.at[13 + n], mrecv.at[13 + n], c=mate).wait_recv()
+
+    relays, onward = [], []
+    for n in range(2):
+        hop(n, ym, n)
+        onward.append(m_copy(9 + n, shard(ym, c, n), shard(ym, c, n), y=yp))
+        onward[-1].start()
+        relay(n, ym, n)
+        hop(7 - n, yp, 3 - n)
+        onward.append(m_copy(11 + n, shard(yp, c, 3 - n), shard(yp, c, 3 - n), y=ym))
+        onward[-1].start()
+        relay(7 - n, yp, 3 - n)
 
     def r_wait(k):
         xx = lax.rem(x + k, NX)
@@ -174,63 +200,48 @@
             vv[j, :, cols] = first * before
             before = before * total
 
-    def hop(n, yy, half):
-        return remote(shard(yy, c, half), shard(yy, c, half), msend.at[n], mrecv.at[n], y=yp)
-
-    def relay(n, yy, half):
-        return m_copy(7 + n, shard(yy, c, half), shard(yy, c, half), c=mate)
-
-    def relayed(n, yy, half):
-        remote(shard(yy, mate, half), shard(yy, mate, half), msend.at[7 + n], mrecv.at[7 + n], c=mate).wait_recv()
-
-    relays = [relay(0, ym, 0), relay(1, yp, 1), relay(2, ym, 1), relay(3, yp, 0), relay(4, y2, 0), relay(5, y2, 1)]
-    up2 = m_copy(5, shard(ym, c, 0), shard(ym, c, 0), y=yp)
-    down2 = m_copy(6, shard(yp, c, 1), shard(yp, c, 1), y=ym)
-
-    def product(yy, first):
-        at = pl.ds(pl.multiple_of(yy * 256, 256), 256)
+    pl.semaphore_wait(met.at[1], 2)
+    along_z(met.at[2], 4)
+
+    def product(row, depth, first=False):
+        at = pl.ds(pl.multiple_of(row, depth), depth)
         left = jnp.concatenate([er[j, :, at] for j in range(NX)], axis=0)
         for k in range(4):
             cols = pl.ds(k * 256, 256)
             term = jnp.dot(left, mb[at, cols], preferred_element_type=f32)
             acc[:, cols] = term if first else acc[:, cols] + term
 
-    hop(0, ym, 0).wait_recv()
-    up2.start()
-    relays[0].start()
-    hop(3, yp, 1).wait_recv()
-    down2.start()
-    relays[1].start()
+    for n in range(2, 4):
+        hop(n, ym, n)
+        relay(n, ym, n)
+        hop(7 - n, yp, 3 - n)
+        relay(7 - n, yp, 3 - n)
     e_own.wait()
     for k in range(1, NX):
         xx = lax.rem(x + k, NX)
         remote(es.at[xx], er.at[xx], esend.at[k - 1], erecv.at[xx], x=xx).wait_recv()
-    remote(m_in, mb.at[pl.ds(pl.multiple_of((y * 2 + mate) * 128, 128), 128), :], msend.at[4], mrecv.at[4], c=mate).wait_recv()
-    product(y, True)
-    pl.semaphore_wait(met.at[0], 2)
-    along_z(met.at[1], 2)
-    hop(1, ym, 1).wait_recv()
-    relays[2].start()
-    hop(2, yp, 0).wait_recv()
-    relays[3].start()
-    relayed(0, ym, 0)
-    relayed(2, ym, 1)
-    product(ym, False)
-    pl.semaphore_wait(met.at[1], 2)
-    along_z(met.at[2], 4)
-    hop(5, y2, 0).wait_recv()
-    relays[4].start()
-    hop(6, y2, 1).wait_recv()
-    relays[5].start()
-    relayed(1, yp, 1)
-    relayed(3, yp, 0)
-    product(yp, False)
+    remote(m_in, mb.at[pl.ds(pl.multiple_of((y * 2 + mate) * 128, 128), 128), :], msend.at[8], mrecv.at[8], c=mate).wait_recv()
+    product(y * 256, 256, True)
     pl.semaphore_wait(met.at[2], 2)
+    for k in range(1, NX):
+        pl.semaphore_signal(met.at[3], inc=1, device_id={"x": lax.rem(x + k, NX)}, device_id_type=MESH_ID)
     for k in FAR_FIRST:
         later(k, lambda k: lr_copy(k).start())
-    relayed(4, y2, 0)
-    relayed(5, y2, 1)
-    product(y2, False)
+    for n in range(2):
+        hop(9 + n, y2, n)
+        relay(8 + n, y2, n)
+        hop(11 + n, y2, 3 - n)
+        relay(11 - n, y2, 3 - n)
+    for n in range(4):
+        relayed(n, ym, n)
+    product(ym * 256, 256)
+    for n in range(4):
+        relayed(4 + n, yp, n)
+    product(yp * 256, 256)
+    product((y2 * 2 + c) * 128, 128)
+    for n in range(4):
+        relayed(8 + n, y2, n)
+    product((y2 * 2 + mate) * 128, 128)
 
     @pl.loop(0, F // LANES)
     def _(k):
@@ -313,43 +324,33 @@
     fs[1:2, :] = base[0:1]
     fs[2:3, :] = top
     fs[3:4, :] = top
-    fr[pl.ds(z, 1)] = fs[...][None]
-
-    def f_copy(k):
-        return remote(fs, fr.at[z], fsend.at[k], frecv.at[z], z=lax.rem(z + k, NZ))
-
-    for k in FAR_FIRST:
-        f_copy(k).start()
-    for k in reversed(FAR_FIRST):
-        u = lax.rem(z + k, NZ)
-        remote(fs, fr.at[u], fsend.at[k], frecv.at[u], z=u).wait_recv()
-
-    passed = jnp.zeros((1, LANES), f32)
-    value = jnp.zeros((1, LANES), f32)
-    for u in range(NZ):
-        value = value + jnp.exp(fr[u, 2:3] - (1.0 / 256.0) * passed) * fr[u, 0:1]
-        passed = passed + fr[u, 1:2]
-    gs[...] = jnp.broadcast_to(value * (1.0 / 4096.0), (8, LANES))
-    g_copies = []
-    for k in range(1, NX):
-        xx = lax.rem(x + k, NX)
-        g_copies.append(remote(gs, gr.at[x], gsend.at[k - 1], grecv.at[x], x=xx))
-        g_copies[-1].start()
-    gr[pl.ds(x, 1)] = gs[...][None]
-
-    for copy in (*up, *down, across, up2, down2, *relays, *r_copies, *e_copies):
+    mine = z * NX + x
+    fr[pl.ds(mine, 1)] = fs[...][None]
+
+    pl.semaphore_wait(met.at[3], NX - 1)
+    for k in (*FAR_FIRST, 0):
+        for n in (2, 1, 3, 0):
+            if k or n:
+                remote(
+                    fs, fr.at[mine], fsend.at[0], frecv.at[0], z=lax.rem(z + k, NZ), x=lax.rem(x + n, NX)
+                ).start()
+
+    for copy in (*up, *down, across, *onward, *relays, *r_copies, *e_copies):
         copy.wait_send()
     for k in FAR_FIRST:
         later(k, lambda k: lr_copy(k).wait_send())
         later(k, lambda k: eb_copy(k).wait_send())
-        f_copy(k).wait_send()
-    for k in range(1, NX):
-        xx = lax.rem(x + k, NX)
-        remote(gs, gr.at[xx], gsend.at[k - 1], grecv.at[xx], x=xx).wait_recv()
-    for j in range(NX):
-        out[j : j + 1, :] = gr[j, 0:1]
-    for copy in g_copies:
-        copy.wait_send()
+    others = fr.at[pl.ds(0, NZ * NX - 1)]
+    everyone = remote(others, others, fsend.at[0], frecv.at[0], z=lax.rem(z + 1, NZ))
+    everyone.wait_recv()
+    passed = jnp.zeros((NX, LANES), f32)
+    value = jnp.zeros((NX, LANES), f32)
+    for u in range(NZ):
+        part = [jnp.concatenate([fr[u * NX + j, r : r + 1] for j in range(NX)], axis=0) for r in range(3)]
+        value = value + jnp.exp(part[2] - (1.0 / 256.0) * passed) * part[0]
+        passed = passed + part[1]
+    out[...] = value * (1.0 / 4096.0)
+    everyone.wait_send()
 
 
 def local(e, s0, m, lp, reg, pay, sc):
@@ -387,18 +388,15 @@
             vmem((NZ, 8, LANES), f32),
             vmem((8, LANES), f32),
             vmem((4, LANES), f32),
-            vmem((NZ, 4, LANES), f32),
-            vmem((8, LANES), f32),
-            vmem((NX, 8, LANES), f32),
+            vmem((NZ * NX, 4, LANES), f32),
             dma((9,)),
-            dma((13,)), dma((13,)),
+            dma((25,)), dma((25,)),
             dma((NX,)), dma((NX,)),
             dma((NX,)), dma((NX,)),
             dma((NZ,)), dma((NZ,)),
             dma((NZ,)), dma((NZ,)),
-            dma((NZ,)), dma((NZ,)),
-            dma((NX,)), dma((NX,)),
-            pltpu.SemaphoreType.REGULAR((3,)),
+            dma((1,)), dma((1,)),
+            pltpu.SemaphoreType.REGULAR((4,)),
         ],
         compiler_params=pltpu.CompilerParams(collective_id=0, has_side_effects=True, vmem_limit_bytes=60 << 20),
         name="scenarios",

time: 51.4 us -> 46.4 us (0.903)
  Pallas kernels: 49.4 us -> 45 us
    pallas_call x1, Pallas kernels: 49.4 us -> 45 us  [local(): pl.pallas_call(kernel, out_shape=jax.ShapeDtypeStruct((PATHS, K), f32), i...]
where the time goes in v3:
time: 46.4 us; the launch traced here: 46.2 us
  Pallas kernels  45 us (97%)
  local copies, waits for them, and re-layouts  1.26 us (3%)
    pallas_call x1, Pallas kernels, local(): pl.pallas_call(kernel, out_shape=jax.ShapeDtypeStruct((PATHS, K), f32), i...  45 us
    unnamed x1, local copies, waits for them, and re-layouts  1.26 us

profile of v3, /device:TPU:1, one launch (start us, length us, event | category | flops | bytes accessed | tf_op | source)
XLA Modules:
  0.0 46.2 jit_solution(4549993034773790828)
XLA Ops:
  0.0 45.0 %scenarios.1 = f32[4,128]{1,0:T(4,128)} custom-call(bf16[64,4,1024]{2,1,0:T(4,128)(2,1)} %e_in.1, f32[4,1024]{1,0:T(4,128)} %s0_in.1, bf16[128,1024]{1,0:T(8,128)(2,1)} %m_in.1, f32[1,1024]{1,0:T(1,128)} %bitcast.4, f32[8,128]{1,0:T(8,128)} %bitcast.5, f32[1,64]{1,0:T(1,128)} %bitcast.7, bf16[1024,128]{1,0:T(8,128)(2,1)} %pay_in.1, bf16[8,128]{1,0:T(8,128)(2,1)} %bitcast.6), custom_call_target="tpu_custom_call" | custom-call | tf_op jit(solution)/shard_map/scenarios/pallas_call | solution.py:358
  45.0 1.3 %copy.9 = f32[4,128]{1,0:T(4,128)} copy(f32[4,128]{1,0:T(4,128)} %scenarios.1) | data formatting | bytes 4096

commit v4 on v3

--- a/solution.py
+++ b/solution.py
@@ -48,8 +48,17 @@
     def shard(yy, cc, piece):
         return mb.at[pl.ds(pl.multiple_of((yy * 2 + cc) * 128 + piece * PIECE, PIECE), PIECE), :]
 
+    turn = (y, ym, yp, y2)
+    width = F // NY
+
+    def quarter(yy):
+        return pl.ds(pl.multiple_of(yy * width, width), width)
+
+    shocks = [
+        pltpu.make_async_copy(e_in.at[:, :, quarter(yy)], ev.at[:, :, quarter(yy)], ld.at[9 + n])
+        for n, yy in enumerate(turn)
+    ]
     loads = [
-        pltpu.make_async_copy(e_in, ev, ld.at[0]),
         pltpu.make_async_copy(reg_in, regv, ld.at[1]),
         pltpu.make_async_copy(lp_in, lpv, ld.at[2]),
         pltpu.make_async_copy(lpd_in, lpd, ld.at[3]),
@@ -58,7 +67,7 @@
         pltpu.make_async_copy(pay_in, bm.at[:, pl.ds(0, K)], ld.at[6]),
         pltpu.make_async_copy(m_in, mb.at[pl.ds(pl.multiple_of((y * 2 + c) * 128, 128), 128), :], ld.at[7]),
     ]
-    for copy in loads:
+    for copy in (*shocks, *loads):
         copy.start()
 
     barrier = pltpu.get_barrier_semaphore()
@@ -73,54 +82,65 @@
 
     along_z(barrier, 1)
 
+    pl.semaphore_wait(barrier, len(peers) + 2)
+    along_z(met.at[0], 1)
+
+    def m_copy(n, src, dst, **where):
+        return remote(src, dst, msend.at[n], mrecv.at[n], **where)
+
+    def own(piece):
+        return m_in.at[pl.ds(piece * PIECE, PIECE), :]
+
+    up = [m_copy(n, own(n), shard(y, c, n), y=yp) for n in range(4)]
+    down = [m_copy(4 + n, own(n), shard(y, c, n), y=ym) for n in range(4)]
+    across = m_copy(8, m_in, mb.at[pl.ds(pl.multiple_of((y * 2 + c) * 128, 128), 128), :], c=mate)
+    for n in range(4):
+        up[n].start()
+        down[3 - n].start()
+    across.start()
+
     loads[0].wait()
+    rw[pl.ds(x, 1)] = jnp.ones((1, 8, LANES), f32)
+    rw[pl.ds(x, 1), :, pl.ds(0, DAYS)] = jnp.broadcast_to(regv[...][None], (1, 8, DAYS))
+    r_copies, e_copies = [], []
+    for k in range(1, NX):
+        xx = lax.rem(x + k, NX)
+        r_copies.append(remote(rw.at[x], rw.at[x], rsend.at[k - 1], rrecv.at[x], x=xx))
+        r_copies[-1].start()
+
     row = lax.broadcasted_iota(jnp.int32, (256, 256), 0)
     col = lax.broadcasted_iota(jnp.int32, (256, 256), 1)
     source = (((row & 7) * 8 + ((row >> 3) & 7)) << 2) + (row >> 6)
     order = (col == source).astype(f32).astype(bf16)
-    for k in range(4):
-        cols = pl.ds(k * 256, 256)
-        flat = ev[:, :, cols].reshape(DAYS * PATHS, 256)
+    e_own = []
+    for n, yy in enumerate(turn):
+        cols = quarter(yy)
+        shocks[n].wait()
+        flat = ev[:, :, cols].reshape(DAYS * PATHS, width)
         moved = jnp.dot(order, flat, preferred_element_type=f32).astype(bf16)
         for p in range(PATHS):
             es[p, :, cols] = moved[p * DAYS : (p + 1) * DAYS]
-    loads[1].wait()
-    rw[pl.ds(x, 1)] = jnp.ones((1, 8, LANES), f32)
-    rw[pl.ds(x, 1), :, pl.ds(0, DAYS)] = jnp.broadcast_to(regv[...][None], (1, 8, DAYS))
-
-    pl.semaphore_wait(barrier, len(peers) + 2)
-    along_z(met.at[0], 1)
-
-    def m_copy(n, src, dst, **where):
-        return remote(src, dst, msend.at[n], mrecv.at[n], **where)
-
-    def own(piece):
-        return m_in.at[pl.ds(piece * PIECE, PIECE), :]
-
-    up = [m_copy(n, own(n), shard(y, c, n), y=yp) for n in range(4)]
-    down = [m_copy(4 + n, own(n), shard(y, c, n), y=ym) for n in range(4)]
-    across = m_copy(8, m_in, mb.at[pl.ds(pl.multiple_of((y * 2 + c) * 128, 128), 128), :], c=mate)
-    r_copies, e_copies = [], []
-    for k in range(1, NX):
-        xx = lax.rem(x + k, NX)
-        r_copies.append(remote(rw.at[x], rw.at[x], rsend.at[k - 1], rrecv.at[x], x=xx))
-        e_copies.append(remote(es.at[xx], er.at[x], esend.at[k - 1], erecv.at[x], x=xx))
-    up[0].start()
-    down[3].start()
-    for copy in r_copies:
-        copy.start()
-    for copy in e_copies:
-        copy.start()
-    for n in (1, 2, 3):
-        up[n].start()
-        down[3 - n].start()
-    across.start()
-    e_own = pltpu.make_async_copy(es.at[x], er.at[x], ld.at[8])
-    e_own.start()
+        for k in (2, 1, 3):
+            xx = lax.rem(x + k, NX)
+            e_copies.append(
+                remote(es.at[xx, :, cols], er.at[x, :, cols], esend.at[n, k - 1], erecv.at[n, x], x=xx)
+            )
+            e_copies[-1].start()
+        e_own.append(pltpu.make_async_copy(es.at[x, :, cols], er.at[x, :, cols], ld.at[13 + n]))
+        e_own[-1].start()
+
+    def shocks_here(n):
+        cols = quarter(turn[n])
+        e_own[n].wait()
+        for k in range(1, NX):
+            xx = lax.rem(x + k, NX)
+            remote(
+                es.at[xx, :, cols], er.at[xx, :, cols], esend.at[n, k - 1], erecv.at[n, xx], x=xx
+            ).wait_recv()
 
     pl.semaphore_wait(met.at[0], 2)
     along_z(met.at[1], 2)
-    for copy in loads[2:]:
+    for copy in loads[1:]:
         copy.wait()
 
     short = scv[...].astype(f32)
@@ -216,11 +236,8 @@
         relay(n, ym, n)
         hop(7 - n, yp, 3 - n)
         relay(7 - n, yp, 3 - n)
-    e_own.wait()
-    for k in range(1, NX):
-        xx = lax.rem(x + k, NX)
-        remote(es.at[xx], er.at[xx], esend.at[k - 1], erecv.at[xx], x=xx).wait_recv()
     remote(m_in, mb.at[pl.ds(pl.multiple_of((y * 2 + mate) * 128, 128), 128), :], msend.at[8], mrecv.at[8], c=mate).wait_recv()
+    shocks_here(0)
     product(y * 256, 256, True)
     pl.semaphore_wait(met.at[2], 2)
     for k in range(1, NX):
@@ -234,10 +251,13 @@
         relay(11 - n, y2, 3 - n)
     for n in range(4):
         relayed(n, ym, n)
+    shocks_here(1)
     product(ym * 256, 256)
     for n in range(4):
         relayed(4 + n, yp, n)
+    shocks_here(2)
     product(yp * 256, 256)
+    shocks_here(3)
     product((y2 * 2 + c) * 128, 128)
     for n in range(4):
         relayed(8 + n, y2, n)
@@ -321,9 +341,8 @@
     for n, power in enumerate(exponent):
         worth = worth + jnp.exp(power - top) * res[pl.ds(n * 8, 8), pl.ds(0, K)]
     fs[0:1, :] = jnp.sum(worth, axis=0, keepdims=True)
-    fs[1:2, :] = base[0:1]
-    fs[2:3, :] = top
-    fs[3:4, :] = top
+    low = lax.broadcasted_iota(jnp.int32, (1, LANES), 1) < LANES // 2
+    fs[1:2, :] = jnp.where(low, base[0:1], top)
     mine = z * NX + x
     fr[pl.ds(mine, 1)] = fs[...][None]
 
@@ -346,9 +365,12 @@
     passed = jnp.zeros((NX, LANES), f32)
     value = jnp.zeros((NX, LANES), f32)
     for u in range(NZ):
-        part = [jnp.concatenate([fr[u * NX + j, r : r + 1] for j in range(NX)], axis=0) for r in range(3)]
-        value = value + jnp.exp(part[2] - (1.0 / 256.0) * passed) * part[0]
-        passed = passed + part[1]
+        part, both = (
+            jnp.concatenate([fr[u * NX + j, r : r + 1] for j in range(NX)], axis=0) for r in range(2)
+        )
+        swapped = pltpu.roll(both, LANES // 2, 1)
+        value = value + jnp.exp(jnp.where(low, swapped, both) - (1.0 / 256.0) * passed) * part
+        passed = passed + jnp.where(low, both, swapped)
     out[...] = value * (1.0 / 4096.0)
     everyone.wait_send()
 
@@ -387,20 +409,25 @@
             vmem((8, LANES), f32),
             vmem((NZ, 8, LANES), f32),
             vmem((8, LANES), f32),
-            vmem((4, LANES), f32),
-            vmem((NZ * NX, 4, LANES), f32),
-            dma((9,)),
+            vmem((2, LANES), f32),
+            vmem((NZ * NX, 2, LANES), f32),
+            dma((17,)),
             dma((25,)), dma((25,)),
-            dma((NX,)), dma((NX,)),
+            dma((NY, NX)), dma((NY, NX)),
             dma((NX,)), dma((NX,)),
             dma((NZ,)), dma((NZ,)),
             dma((NZ,)), dma((NZ,)),
             dma((1,)), dma((1,)),
             pltpu.SemaphoreType.REGULAR((4,)),
         ],
-        compiler_params=pltpu.CompilerParams(collective_id=0, has_side_effects=True, vmem_limit_bytes=60 << 20),
+        compiler_params=pltpu.CompilerParams(collective_id=0, has_side_effects=True, vmem_limit_bytes=32 << 20),
         name="scenarios",
-    )(e, s0, m, lp.reshape(1, F), lp.reshape(8, LANES), reg.reshape(1, DAYS), pay, sc.reshape(8, LANES))
+    )(
+        *(
+            pltpu.with_memory_space_constraint(a, pltpu.HBM)
+            for a in (e, s0, m, lp.reshape(1, F), lp.reshape(8, LANES), reg.reshape(1, DAYS), pay, sc.reshape(8, LANES))
+        )
+    )
 
 
 def solution(mesh):

time: 46.4 us -> 43.8 us (0.944)
  Pallas kernels: 45 us -> 43.1 us
  local copies, waits for them, and re-layouts: 1.26 us -> 0.58 us
    pallas_call x1, Pallas kernels: 45 us -> 43.1 us  [local(): pl.pallas_call(kernel, out_shape=jax.ShapeDtypeStruct((PATHS, K), f32), i...]
    unnamed x1, local copies, waits for them, and re-layouts: 1.26 us -> 0.58 us
where the time goes in v4:
time: 43.8 us; the launch traced here: 43.7 us
  Pallas kernels  43.1 us (98%)
  local copies, waits for them, and re-layouts  0.58 us (1%)
    pallas_call x1, Pallas kernels, local(): pl.pallas_call(kernel, out_shape=jax.ShapeDtypeStruct((PATHS, K), f32), i...  43.1 us

profile of v4, /device:TPU:1, one launch (start us, length us, event | category | flops | bytes accessed | tf_op | source)
XLA Modules:
  0.0 43.7 jit_solution(5662702614370207155)
XLA Ops:
  0.0 43.1 %scenarios.1 = f32[4,128]{1,0:T(4,128)S(1)} custom-call(bf16[64,4,1024]{2,1,0:T(4,128)(2,1)} %e_in.1, f32[4,1024]{1,0:T(4,128)} %s0_in.1, bf16[128,1024]{1,0:T(8,128)(2,1)} %m_in.1, f32[1,1024]{1,0:T(1,128)} %bitcast.4, f32[8,128]{1,0:T(8,128)} %bitcast.5, f32[1,64]{1,0:T(1,128)} %bitcast.7, bf16[1024,128]{1,0:T(8,128)(2,1)} %pay_in.1, bf16[8,128]{1,0:T(8,128)(2,1)} %bitcast.6), custom_call_target="tpu_custom_call" | custom-call | tf_op jit(solution)/shard_map/scenarios/pallas_call | solution.py:380
  43.1 0.6 %copy.9 = f32[4,128]{1,0:T(4,128)} copy(f32[4,128]{1,0:T(4,128)S(1)} %scenarios.1) | data formatting | bytes 4096

commit v5 on v4

--- a/solution.py
+++ b/solution.py
@@ -71,8 +71,8 @@
         copy.start()
 
     barrier = pltpu.get_barrier_semaphore()
-    peers = [{"c": mate}, {"y": yp}, {"y": ym}]
-    peers += [{"x": lax.rem(x + k, NX)} for k in range(1, NX)]
+    beside = [{"x": lax.rem(x + k, NX)} for k in (1, NX - 1)]
+    peers = [{"c": mate}, {"y": yp}, {"y": ym}, *beside]
     for peer in peers:
         pl.semaphore_signal(barrier, inc=1, device_id=peer, device_id_type=MESH_ID)
 
@@ -85,28 +85,31 @@
     pl.semaphore_wait(barrier, len(peers) + 2)
     along_z(met.at[0], 1)
 
+    for peer in beside:
+        pl.semaphore_signal(met.at[4], inc=1, device_id=peer, device_id_type=MESH_ID)
+
     def m_copy(n, src, dst, **where):
         return remote(src, dst, msend.at[n], mrecv.at[n], **where)
 
+    odd = lax.rem(z, 2)
+    rising = [2 * odd, 2 * odd + 1]
+    falling = [2 - 2 * odd, 3 - 2 * odd]
+
     def own(piece):
-        return m_in.at[pl.ds(piece * PIECE, PIECE), :]
-
-    up = [m_copy(n, own(n), shard(y, c, n), y=yp) for n in range(4)]
-    down = [m_copy(4 + n, own(n), shard(y, c, n), y=ym) for n in range(4)]
-    across = m_copy(8, m_in, mb.at[pl.ds(pl.multiple_of((y * 2 + c) * 128, 128), 128), :], c=mate)
-    for n in range(4):
-        up[n].start()
-        down[3 - n].start()
-    across.start()
+        return m_in.at[pl.ds(pl.multiple_of(piece * PIECE, PIECE), PIECE), :]
+
+    straight = []
+    for n in range(2):
+        straight.append(m_copy(n, own(rising[n]), shard(y, c, rising[n]), y=yp))
+        straight.append(m_copy(2 + n, own(falling[n]), shard(y, c, falling[n]), y=ym))
+    straight.append(m_copy(4, m_in, mb.at[pl.ds(pl.multiple_of((y * 2 + c) * 128, 128), 128), :], c=mate))
+    for copy in straight:
+        copy.start()
 
     loads[0].wait()
     rw[pl.ds(x, 1)] = jnp.ones((1, 8, LANES), f32)
     rw[pl.ds(x, 1), :, pl.ds(0, DAYS)] = jnp.broadcast_to(regv[...][None], (1, 8, DAYS))
     r_copies, e_copies = [], []
-    for k in range(1, NX):
-        xx = lax.rem(x + k, NX)
-        r_copies.append(remote(rw.at[x], rw.at[x], rsend.at[k - 1], rrecv.at[x], x=xx))
-        r_copies[-1].start()
 
     row = lax.broadcasted_iota(jnp.int32, (256, 256), 0)
     col = lax.broadcasted_iota(jnp.int32, (256, 256), 1)
@@ -120,6 +123,12 @@
         moved = jnp.dot(order, flat, preferred_element_type=f32).astype(bf16)
         for p in range(PATHS):
             es[p, :, cols] = moved[p * DAYS : (p + 1) * DAYS]
+        if n == 0:
+            pl.semaphore_wait(met.at[4], 2)
+            for k in (2, 1, 3):
+                xx = lax.rem(x + k, NX)
+                r_copies.append(remote(rw.at[x], rw.at[x], rsend.at[k - 1], rrecv.at[x], x=xx))
+                r_copies[-1].start()
         for k in (2, 1, 3):
             xx = lax.rem(x + k, NX)
             e_copies.append(
@@ -138,6 +147,28 @@
                 es.at[xx, :, cols], er.at[xx, :, cols], esend.at[n, k - 1], erecv.at[n, xx], x=xx
             ).wait_recv()
 
+    def hop(n, yy, piece):
+        remote(shard(yy, c, piece), shard(yy, c, piece), msend.at[n], mrecv.at[n], y=yp).wait_recv()
+
+    def passed_on(n, yy, piece, **where):
+        onward.append(m_copy(n, shard(yy, c, piece), shard(yy, c, piece), **where))
+        onward[-1].start()
+
+    def relayed(n, yy, piece):
+        remote(shard(yy, mate, piece), shard(yy, mate, piece), msend.at[n], mrecv.at[n], c=mate).wait_recv()
+
+    onward = []
+    aside = [{"z": lax.rem(z + 1, NZ)}, {"z": lax.rem(z + NZ - 1, NZ)}]
+    for n in range(2):
+        hop(n, ym, rising[n])
+        passed_on(5 + n, ym, rising[n], y=yp)
+        passed_on(9 + n, ym, rising[n], **aside[n])
+        passed_on(13 + n, ym, rising[n], c=mate)
+        hop(2 + n, yp, falling[n])
+        passed_on(7 + n, yp, falling[n], y=ym)
+        passed_on(11 + n, yp, falling[n], **aside[n])
+        passed_on(15 + n, yp, falling[n], c=mate)
+
     pl.semaphore_wait(met.at[0], 2)
     along_z(met.at[1], 2)
     for copy in loads[1:]:
@@ -147,27 +178,6 @@
     for k in range(F // LANES):
         block = jnp.broadcast_to(short[k : k + 1], (LANES, LANES))
         bm[pl.ds(k * LANES, LANES), pl.ds(K, LANES)] = block.T.astype(bf16)
-
-    def hop(n, yy, piece):
-        remote(shard(yy, c, piece), shard(yy, c, piece), msend.at[n], mrecv.at[n], y=yp).wait_recv()
-
-    def relay(n, yy, piece):
-        relays.append(m_copy(13 + n, shard(yy, c, piece), shard(yy, c, piece), c=mate))
-        relays[-1].start()
-
-    def relayed(n, yy, piece):
-        remote(shard(yy, mate, piece), shard(yy, mate, piece), msend.at[13 + n], mrecv.at[13 + n], c=mate).wait_recv()
-
-    relays, onward = [], []
-    for n in range(2):
-        hop(n, ym, n)
-        onward.append(m_copy(9 + n, shard(ym, c, n), shard(ym, c, n), y=yp))
-        onward[-1].start()
-        relay(n, ym, n)
-        hop(7 - n, yp, 3 - n)
-        onward.append(m_copy(11 + n, shard(yp, c, 3 - n), shard(yp, c, 3 - n), y=ym))
-        onward[-1].start()
-        relay(7 - n, yp, 3 - n)
 
     def r_wait(k):
         xx = lax.rem(x + k, NX)
@@ -231,37 +241,39 @@
             term = jnp.dot(left, mb[at, cols], preferred_element_type=f32)
             acc[:, cols] = term if first else acc[:, cols] + term
 
-    for n in range(2, 4):
-        hop(n, ym, n)
-        relay(n, ym, n)
-        hop(7 - n, yp, 3 - n)
-        relay(7 - n, yp, 3 - n)
-    remote(m_in, mb.at[pl.ds(pl.multiple_of((y * 2 + mate) * 128, 128), 128), :], msend.at[8], mrecv.at[8], c=mate).wait_recv()
-    shocks_here(0)
-    product(y * 256, 256, True)
+    for n in range(2):
+        hop(9 + n, ym, falling[n])
+        passed_on(17 + n, ym, falling[n], c=mate)
+        hop(11 + n, yp, rising[n])
+        passed_on(19 + n, yp, rising[n], c=mate)
+    for n in range(2):
+        hop(5 + n, y2, rising[n])
+        passed_on(21 + n, y2, rising[n], c=mate)
+        hop(7 + n, y2, falling[n])
+        passed_on(23 + n, y2, falling[n], c=mate)
     pl.semaphore_wait(met.at[2], 2)
     for k in range(1, NX):
         pl.semaphore_signal(met.at[3], inc=1, device_id={"x": lax.rem(x + k, NX)}, device_id_type=MESH_ID)
     for k in FAR_FIRST:
         later(k, lambda k: lr_copy(k).start())
-    for n in range(2):
-        hop(9 + n, y2, n)
-        relay(8 + n, y2, n)
-        hop(11 + n, y2, 3 - n)
-        relay(11 - n, y2, 3 - n)
-    for n in range(4):
-        relayed(n, ym, n)
+    remote(m_in, mb.at[pl.ds(pl.multiple_of((y * 2 + mate) * 128, 128), 128), :], msend.at[4], mrecv.at[4], c=mate).wait_recv()
+    shocks_here(0)
+    product(y * 256, 256, True)
+    for n in range(2):
+        relayed(13 + n, ym, rising[n])
+        relayed(17 + n, ym, falling[n])
     shocks_here(1)
     product(ym * 256, 256)
-    for n in range(4):
-        relayed(4 + n, yp, n)
+    for n in range(2):
+        relayed(15 + n, yp, falling[n])
+        relayed(19 + n, yp, rising[n])
     shocks_here(2)
     product(yp * 256, 256)
+    for n in range(2):
+        relayed(21 + n, y2, rising[n])
+        relayed(23 + n, y2, falling[n])
     shocks_here(3)
-    product((y2 * 2 + c) * 128, 128)
-    for n in range(4):
-        relayed(8 + n, y2, n)
-    product((y2 * 2 + mate) * 128, 128)
+    product(y2 * 256, 256)
 
     @pl.loop(0, F // LANES)
     def _(k):
@@ -354,7 +366,7 @@
                     fs, fr.at[mine], fsend.at[0], frecv.at[0], z=lax.rem(z + k, NZ), x=lax.rem(x + n, NX)
                 ).start()
 
-    for copy in (*up, *down, across, *onward, *relays, *r_copies, *e_copies):
+    for copy in (*straight, *onward, *r_copies, *e_copies):
         copy.wait_send()
     for k in FAR_FIRST:
         later(k, lambda k: lr_copy(k).wait_send())
@@ -418,7 +430,7 @@
             dma((NZ,)), dma((NZ,)),
             dma((NZ,)), dma((NZ,)),
             dma((1,)), dma((1,)),
-            pltpu.SemaphoreType.REGULAR((4,)),
+            pltpu.SemaphoreType.REGULAR((5,)),
         ],
         compiler_params=pltpu.CompilerParams(collective_id=0, has_side_effects=True, vmem_limit_bytes=32 << 20),
         name="scenarios",

time: 43.8 us -> 44.7 us (1.021)
  the two profiles are of different devices: /device:TPU:1 before, /device:TPU:32 now
where the time goes in v5:
time: 44.7 us; the launch traced here: 44.6 us
  Pallas kernels  44 us (98%)
  local copies, waits for them, and re-layouts  0.58 us (1%)
    pallas_call x1, Pallas kernels, local(): pl.pallas_call(kernel, out_shape=jax.ShapeDtypeStruct((PATHS, K), f32), i...  44 us

profile of v5, /device:TPU:32, one launch (start us, length us, event | category | flops | bytes accessed | tf_op | source)
XLA Modules:
  0.0 44.6 jit_solution(5696162120318867577)
XLA Ops:
  0.0 44.0 %scenarios.1 = f32[4,128]{1,0:T(4,128)S(1)} custom-call(bf16[64,4,1024]{2,1,0:T(4,128)(2,1)} %e_in.1, f32[4,1024]{1,0:T(4,128)} %s0_in.1, bf16[128,1024]{1,0:T(8,128)(2,1)} %m_in.1, f32[1,1024]{1,0:T(1,128)} %bitcast.4, f32[8,128]{1,0:T(8,128)} %bitcast.5, f32[1,64]{1,0:T(1,128)} %bitcast.7, bf16[1024,128]{1,0:T(8,128)(2,1)} %pay_in.1, bf16[8,128]{1,0:T(8,128)(2,1)} %bitcast.6), custom_call_target="tpu_custom_call" | custom-call | tf_op jit(solution)/shard_map/scenarios/pallas_call | solution.py:392
  44.0 0.6 %copy.9 = f32[4,128]{1,0:T(4,128)} copy(f32[4,128]{1,0:T(4,128)S(1)} %scenarios.1) | data formatting | bytes 4096

commit v6 on v5

--- a/solution.py
+++ b/solution.py
@@ -12,7 +12,8 @@
 NY, NC, NZ, NX = 4, 2, 16, 4
 DAYS, PATHS, F, K = 64, 4, 1024, 128
 BLOCK = DAYS * NX
-PIECE = 32
+PIECE = 16
+HALF = 64 // PIECE
 LANES = 128
 FAR_FIRST = (8, 7, 9, 6, 10, 5, 11, 4, 12, 3, 13, 2, 14, 1, 15)
 f32, bf16 = jnp.float32, jnp.bfloat16
@@ -37,13 +38,25 @@
 
 def kernel(
     e_in, s0_in, m_in, lp_in, lpd_in, reg_in, pay_in, sc_in, out,
-    ev, es, er, mb, bm, acc, dd, scen, res, rw, rb, lpv, lpd, s0v, regv, scv,
+    ev, es, er, mb, bm, acc, dd, res, rw, rb, lpv, lpd, s0v, regv, scv,
     dk, dx, dt, uu, vv, lrs, lrr, ebs, ebr, cbs, fs, fr,
     ld, msend, mrecv, esend, erecv, rsend, rrecv, lsend, lrecv, bsend, brecv, fsend, frecv, met,
 ):
     y, c, z, x = (lax.axis_index(a) for a in ("y", "c", "z", "x"))
     yp, ym, y2 = lax.rem(y + 1, NY), lax.rem(y + NY - 1, NY), lax.rem(y + 2, NY)
     mate = 1 - c
+
+    barrier = pltpu.get_barrier_semaphore()
+    beside = [{"x": lax.rem(x + k, NX)} for k in (1, NX - 1)]
+    peers = [{"c": mate}, {"y": yp}, {"y": ym}, *beside]
+    for peer in peers:
+        pl.semaphore_signal(barrier, inc=1, device_id=peer, device_id_type=MESH_ID)
+
+    def along_z(semaphore, distance):
+        for k in (distance, NZ - distance):
+            pl.semaphore_signal(semaphore, inc=1, device_id={"z": lax.rem(z + k, NZ)}, device_id_type=MESH_ID)
+
+    along_z(barrier, 1)
 
     def shard(yy, cc, piece):
         return mb.at[pl.ds(pl.multiple_of((yy * 2 + cc) * 128 + piece * PIECE, PIECE), PIECE), :]
@@ -70,39 +83,30 @@
     for copy in (*shocks, *loads):
         copy.start()
 
-    barrier = pltpu.get_barrier_semaphore()
-    beside = [{"x": lax.rem(x + k, NX)} for k in (1, NX - 1)]
-    peers = [{"c": mate}, {"y": yp}, {"y": ym}, *beside]
-    for peer in peers:
-        pl.semaphore_signal(barrier, inc=1, device_id=peer, device_id_type=MESH_ID)
-
-    def along_z(semaphore, distance):
-        for k in (distance, NZ - distance):
-            pl.semaphore_signal(semaphore, inc=1, device_id={"z": lax.rem(z + k, NZ)}, device_id_type=MESH_ID)
-
-    along_z(barrier, 1)
-
     pl.semaphore_wait(barrier, len(peers) + 2)
     along_z(met.at[0], 1)
 
     for peer in beside:
         pl.semaphore_signal(met.at[4], inc=1, device_id=peer, device_id_type=MESH_ID)
 
+    def group(g, n):
+        return g * HALF + n
+
     def m_copy(n, src, dst, **where):
         return remote(src, dst, msend.at[n], mrecv.at[n], **where)
 
     odd = lax.rem(z, 2)
-    rising = [2 * odd, 2 * odd + 1]
-    falling = [2 - 2 * odd, 3 - 2 * odd]
+    rising = [HALF * odd + n for n in range(HALF)]
+    falling = [HALF * (1 - odd) + n for n in range(HALF)]
 
     def own(piece):
         return m_in.at[pl.ds(pl.multiple_of(piece * PIECE, PIECE), PIECE), :]
 
     straight = []
-    for n in range(2):
-        straight.append(m_copy(n, own(rising[n]), shard(y, c, rising[n]), y=yp))
-        straight.append(m_copy(2 + n, own(falling[n]), shard(y, c, falling[n]), y=ym))
-    straight.append(m_copy(4, m_in, mb.at[pl.ds(pl.multiple_of((y * 2 + c) * 128, 128), 128), :], c=mate))
+    for n in range(HALF):
+        straight.append(m_copy(group(0, n), own(rising[n]), shard(y, c, rising[n]), y=yp))
+        straight.append(m_copy(group(1, n), own(falling[n]), shard(y, c, falling[n]), y=ym))
+    straight.append(m_copy(group(12, 0), m_in, mb.at[pl.ds(pl.multiple_of((y * 2 + c) * 128, 128), 128), :], c=mate))
     for copy in straight:
         copy.start()
 
@@ -124,6 +128,8 @@
         for p in range(PATHS):
             es[p, :, cols] = moved[p * DAYS : (p + 1) * DAYS]
         if n == 0:
+            pl.semaphore_wait(met.at[0], 2)
+            along_z(met.at[1], 2)
             pl.semaphore_wait(met.at[4], 2)
             for k in (2, 1, 3):
                 xx = lax.rem(x + k, NX)
@@ -138,6 +144,9 @@
         e_own.append(pltpu.make_async_copy(es.at[x, :, cols], er.at[x, :, cols], ld.at[13 + n]))
         e_own[-1].start()
 
+    pl.semaphore_wait(met.at[1], 2)
+    along_z(met.at[2], 4)
+
     def shocks_here(n):
         cols = quarter(turn[n])
         e_own[n].wait()
@@ -159,18 +168,16 @@
 
     onward = []
     aside = [{"z": lax.rem(z + 1, NZ)}, {"z": lax.rem(z + NZ - 1, NZ)}]
-    for n in range(2):
-        hop(n, ym, rising[n])
-        passed_on(5 + n, ym, rising[n], y=yp)
-        passed_on(9 + n, ym, rising[n], **aside[n])
-        passed_on(13 + n, ym, rising[n], c=mate)
-        hop(2 + n, yp, falling[n])
-        passed_on(7 + n, yp, falling[n], y=ym)
-        passed_on(11 + n, yp, falling[n], **aside[n])
-        passed_on(15 + n, yp, falling[n], c=mate)
-
-    pl.semaphore_wait(met.at[0], 2)
-    along_z(met.at[1], 2)
+    for n in range(HALF):
+        hop(group(0, n), ym, rising[n])
+        passed_on(group(2, n), ym, rising[n], y=yp)
+        passed_on(group(4, n), ym, rising[n], **aside[n % 2])
+        passed_on(group(6, n), ym, rising[n], c=mate)
+        hop(group(1, n), yp, falling[n])
+        passed_on(group(3, n), yp, falling[n], y=ym)
+        passed_on(group(5, n), yp, falling[n], **aside[n % 2])
+        passed_on(group(7, n), yp, falling[n], c=mate)
+
     for copy in loads[1:]:
         copy.wait()
 
@@ -230,9 +237,6 @@
             vv[j, :, cols] = first * before
             before = before * total
 
-    pl.semaphore_wait(met.at[1], 2)
-    along_z(met.at[2], 4)
-
     def product(row, depth, first=False):
         at = pl.ds(pl.multiple_of(row, depth), depth)
         left = jnp.concatenate([er[j, :, at] for j in range(NX)], axis=0)
@@ -241,61 +245,64 @@
             term = jnp.dot(left, mb[at, cols], preferred_element_type=f32)
             acc[:, cols] = term if first else acc[:, cols] + term
 
-    for n in range(2):
-        hop(9 + n, ym, falling[n])
-        passed_on(17 + n, ym, falling[n], c=mate)
-        hop(11 + n, yp, rising[n])
-        passed_on(19 + n, yp, rising[n], c=mate)
-    for n in range(2):
-        hop(5 + n, y2, rising[n])
-        passed_on(21 + n, y2, rising[n], c=mate)
-        hop(7 + n, y2, falling[n])
-        passed_on(23 + n, y2, falling[n], c=mate)
+    for n in range(HALF):
+        hop(group(4, n), ym, falling[n])
+        passed_on(group(8, n), ym, falling[n], c=mate)
+        hop(group(5, n), yp, rising[n])
+        passed_on(group(9, n), yp, rising[n], c=mate)
+    for n in range(HALF):
+        hop(group(2, n), y2, rising[n])
+        passed_on(group(10, n), y2, rising[n], c=mate)
+        hop(group(3, n), y2, falling[n])
+        passed_on(group(11, n), y2, falling[n], c=mate)
     pl.semaphore_wait(met.at[2], 2)
     for k in range(1, NX):
         pl.semaphore_signal(met.at[3], inc=1, device_id={"x": lax.rem(x + k, NX)}, device_id_type=MESH_ID)
     for k in FAR_FIRST:
         later(k, lambda k: lr_copy(k).start())
-    remote(m_in, mb.at[pl.ds(pl.multiple_of((y * 2 + mate) * 128, 128), 128), :], msend.at[4], mrecv.at[4], c=mate).wait_recv()
+    remote(m_in, mb.at[pl.ds(pl.multiple_of((y * 2 + mate) * 128, 128), 128), :], msend.at[group(12, 0)], mrecv.at[group(12, 0)], c=mate).wait_recv()
     shocks_here(0)
     product(y * 256, 256, True)
-    for n in range(2):
-        relayed(13 + n, ym, rising[n])
-        relayed(17 + n, ym, falling[n])
+    for n in range(HALF):
+        relayed(group(6, n), ym, rising[n])
+        relayed(group(8, n), ym, falling[n])
     shocks_here(1)
     product(ym * 256, 256)
-    for n in range(2):
-        relayed(15 + n, yp, falling[n])
-        relayed(19 + n, yp, rising[n])
+    for n in range(HALF):
+        relayed(group(7, n), yp, falling[n])
+        relayed(group(9, n), yp, rising[n])
     shocks_here(2)
     product(yp * 256, 256)
-    for n in range(2):
-        relayed(21 + n, y2, rising[n])
-        relayed(23 + n, y2, falling[n])
     shocks_here(3)
-    product(y2 * 256, 256)
-
-    @pl.loop(0, F // LANES)
-    def _(k):
-        cols = columns(k)
-        log_keep = lpv[:, cols]
-        keep = jnp.broadcast_to(jnp.exp(log_keep), (8, LANES))
-        double = 2.0 * log_keep
-        vol = jnp.broadcast_to(jnp.sqrt(-expm1(double)), (8, LANES))
-        carried = jnp.zeros((8, LANES), f32)
-        for j in range(NX):
-            state = None
-            for i in range(8):
-                r = pl.ds(j * DAYS + i * 8, 8)
-                shock = vol * acc[r, cols]
-                state = shock if i == 0 else (keep * rb[r, :]) * state + shock
-                acc[r, cols] = state
-            for n, shift in enumerate((1, 2, 4)):
-                state = state + dk[n, j, :, cols] * pltpu.roll(state, shift, 0)
-            first = jnp.where(sub >= 1, pltpu.roll(state, 1, 0), 0.0)
-            uu[j, :, cols] = first + dx[j, :, cols] * carried
-            carried = dt[j, :, cols] * carried + jnp.broadcast_to(state[7:8], (8, LANES))
-        ebs[pl.ds(k, 1), :] = carried[0:1]
+    for n in range(HALF):
+        relayed(group(10, n), y2, rising[n])
+        relayed(group(11, n), y2, falling[n])
+
+    last = quarter(y2)
+    left = jnp.concatenate([er[j, :, last] for j in range(NX)], axis=0)
+    for w in range(4):
+        wide = pl.ds(w * 256, 256)
+        acc[:, wide] = acc[:, wide] + jnp.dot(left, mb[last, wide], preferred_element_type=f32)
+        for k in (2 * w, 2 * w + 1):
+            cols = pl.ds(k * LANES, LANES)
+            log_keep = lpv[:, cols]
+            keep = jnp.broadcast_to(jnp.exp(log_keep), (8, LANES))
+            double = 2.0 * log_keep
+            vol = jnp.broadcast_to(jnp.sqrt(-expm1(double)), (8, LANES))
+            carried = jnp.zeros((8, LANES), f32)
+            for j in range(NX):
+                state = None
+                for i in range(8):
+                    r = pl.ds(j * DAYS + i * 8, 8)
+                    shock = vol * acc[r, cols]
+                    state = shock if i == 0 else (keep * rb[r, :]) * state + shock
+                    acc[r, cols] = state
+                for n, shift in enumerate((1, 2, 4)):
+                    state = state + dk[n, j, :, cols] * pltpu.roll(state, shift, 0)
+                first = jnp.where(sub >= 1, pltpu.roll(state, 1, 0), 0.0)
+                uu[j, :, cols] = first + dx[j, :, cols] * carried
+                carried = dt[j, :, cols] * carried + jnp.broadcast_to(state[7:8], (8, LANES))
+            ebs[k : k + 1, :] = carried[0:1]
 
     for k in FAR_FIRST:
         later(k, lambda k: eb_copy(k).start())
@@ -326,12 +333,12 @@
 
     cbs[...] = lax.fori_loop(0, z, entered, cbs[...])
 
-    @pl.loop(0, F // LANES)
-    def _(k):
-        cols = columns(k)
-        scen[:, cols] = (acc[:, cols] + dd[:, cols] * cbs[pl.ds(k, 1), :]).astype(bf16)
-
-    res[...] = jnp.dot(scen[...], bm[...], preferred_element_type=f32)
+    for w in range(4):
+        wide = pl.ds(w * 256, 256)
+        now = jnp.concatenate([cbs[k : k + 1, :] for k in (2 * w, 2 * w + 1)], axis=1)
+        scenario = (acc[:, wide] + dd[:, wide] * now).astype(bf16)
+        term = jnp.dot(scenario, bm[wide, :], preferred_element_type=f32)
+        res[...] = term if w == 0 else res[...] + term
 
     base = jnp.zeros((8, LANES), f32)
     exponent = []
@@ -402,7 +409,6 @@
             vmem((F, 2 * K), bf16),
             vmem((BLOCK, F), f32),
             vmem((BLOCK, F), f32),
-            vmem((BLOCK, F), bf16),
             vmem((BLOCK, 2 * K), f32),
             vmem((NX, 8, LANES), f32),
             vmem((BLOCK, LANES), f32),
@@ -424,7 +430,7 @@
             vmem((2, LANES), f32),
             vmem((NZ * NX, 2, LANES), f32),
             dma((17,)),
-            dma((25,)), dma((25,)),
+            dma((12 * HALF + 1,)), dma((12 * HALF + 1,)),
             dma((NY, NX)), dma((NY, NX)),
             dma((NX,)), dma((NX,)),
             dma((NZ,)), dma((NZ,)),

time: 44.7 us -> 43 us (0.962)
  the two profiles are of different devices: /device:TPU:32 before, /device:TPU:1 now
where the time goes in v6:
time: 43 us; the launch traced here: 42.9 us
  Pallas kernels  42.3 us (98%)
  local copies, waits for them, and re-layouts  0.58 us (1%)
    pallas_call x1, Pallas kernels, local(): pl.pallas_call(kernel, out_shape=jax.ShapeDtypeStruct((PATHS, K), f32), i...  42.3 us

profile of v6, /device:TPU:1, one launch (start us, length us, event | category | flops | bytes accessed | tf_op | source)
XLA Modules:
  0.0 42.9 jit_solution(17449851925122056703)
XLA Ops:
  0.0 42.3 %scenarios.1 = f32[4,128]{1,0:T(4,128)S(1)} custom-call(bf16[64,4,1024]{2,1,0:T(4,128)(2,1)} %e_in.1, f32[4,1024]{1,0:T(4,128)} %s0_in.1, bf16[128,1024]{1,0:T(8,128)(2,1)} %m_in.1, f32[1,1024]{1,0:T(1,128)} %bitcast.4, f32[8,128]{1,0:T(8,128)} %bitcast.5, f32[1,64]{1,0:T(1,128)} %bitcast.7, bf16[1024,128]{1,0:T(8,128)(2,1)} %pay_in.1, bf16[8,128]{1,0:T(8,128)(2,1)} %bitcast.6), custom_call_target="tpu_custom_call" | custom-call | tf_op jit(solution)/shard_map/scenarios/pallas_call | solution.py:399
  42.3 0.6 %copy.9 = f32[4,128]{1,0:T(4,128)} copy(f32[4,128]{1,0:T(4,128)S(1)} %scenarios.1) | data formatting | bytes 4096

commit v7 on v6

--- a/solution.py
+++ b/solution.py
@@ -12,8 +12,8 @@
 NY, NC, NZ, NX = 4, 2, 16, 4
 DAYS, PATHS, F, K = 64, 4, 1024, 128
 BLOCK = DAYS * NX
-PIECE = 16
-HALF = 64 // PIECE
+PIECE = 128
+HALF = F // 2 // PIECE
 LANES = 128
 FAR_FIRST = (8, 7, 9, 6, 10, 5, 11, 4, 12, 3, 13, 2, 14, 1, 15)
 f32, bf16 = jnp.float32, jnp.bfloat16
@@ -59,7 +59,9 @@
     along_z(barrier, 1)
 
     def shard(yy, cc, piece):
-        return mb.at[pl.ds(pl.multiple_of((yy * 2 + cc) * 128 + piece * PIECE, PIECE), PIECE), :]
+        return mb.at[
+            pl.ds(pl.multiple_of((yy * 2 + cc) * 128, 128), 128), pl.ds(pl.multiple_of(piece * PIECE, PIECE), PIECE)
+        ]
 
     turn = (y, ym, yp, y2)
     width = F // NY
@@ -100,7 +102,7 @@
     falling = [HALF * (1 - odd) + n for n in range(HALF)]
 
     def own(piece):
-        return m_in.at[pl.ds(pl.multiple_of(piece * PIECE, PIECE), PIECE), :]
+        return m_in.at[:, pl.ds(pl.multiple_of(piece * PIECE, PIECE), PIECE)]
 
     straight = []
     for n in range(HALF):
@@ -172,19 +174,15 @@
         hop(group(0, n), ym, rising[n])
         passed_on(group(2, n), ym, rising[n], y=yp)
         passed_on(group(4, n), ym, rising[n], **aside[n % 2])
-        passed_on(group(6, n), ym, rising[n], c=mate)
         hop(group(1, n), yp, falling[n])
         passed_on(group(3, n), yp, falling[n], y=ym)
         passed_on(group(5, n), yp, falling[n], **aside[n % 2])
+    for n in range(HALF):
+        passed_on(group(6, n), ym, rising[n], c=mate)
         passed_on(group(7, n), yp, falling[n], c=mate)
 
     for copy in loads[1:]:
         copy.wait()
-
-    short = scv[...].astype(f32)
-    for k in range(F // LANES):
-        block = jnp.broadcast_to(short[k : k + 1], (LANES, LANES))
-        bm[pl.ds(k * LANES, LANES), pl.ds(K, LANES)] = block.T.astype(bf16)
 
     def r_wait(k):
         xx = lax.rem(x + k, NX)
@@ -237,13 +235,11 @@
             vv[j, :, cols] = first * before
             before = before * total
 
-    def product(row, depth, first=False):
-        at = pl.ds(pl.multiple_of(row, depth), depth)
-        left = jnp.concatenate([er[j, :, at] for j in range(NX)], axis=0)
-        for k in range(4):
-            cols = pl.ds(k * 256, 256)
-            term = jnp.dot(left, mb[at, cols], preferred_element_type=f32)
-            acc[:, cols] = term if first else acc[:, cols] + term
+    def shocks_of(yy):
+        return jnp.concatenate([er[j, :, quarter(yy)] for j in range(NX)], axis=0)
+
+    def block(half, w):
+        return pl.ds(pl.multiple_of(half[2 * w] * PIECE, 256), 256)
 
     for n in range(HALF):
         hop(group(4, n), ym, falling[n])
@@ -262,47 +258,56 @@
         later(k, lambda k: lr_copy(k).start())
     remote(m_in, mb.at[pl.ds(pl.multiple_of((y * 2 + mate) * 128, 128), 128), :], msend.at[group(12, 0)], mrecv.at[group(12, 0)], c=mate).wait_recv()
     shocks_here(0)
-    product(y * 256, 256, True)
-    for n in range(HALF):
-        relayed(group(6, n), ym, rising[n])
+    left = shocks_of(y)
+    for w in range(4):
+        cols = pl.ds(w * 256, 256)
+        acc[:, cols] = jnp.dot(left, mb[quarter(y), cols], preferred_element_type=f32)
+    early = ((1, ym, rising, 6), (2, yp, falling, 7))
+    for turned, yy, half, g in early:
+        shocks_here(turned)
+        for n in range(HALF):
+            relayed(group(g, n), yy, half[n])
+        left = shocks_of(yy)
+        for w in range(2):
+            cols = block(half, w)
+            acc[:, cols] = acc[:, cols] + jnp.dot(left, mb[quarter(yy), cols], preferred_element_type=f32)
+    shocks_here(3)
+    for n in range(HALF):
         relayed(group(8, n), ym, falling[n])
-    shocks_here(1)
-    product(ym * 256, 256)
-    for n in range(HALF):
-        relayed(group(7, n), yp, falling[n])
         relayed(group(9, n), yp, rising[n])
-    shocks_here(2)
-    product(yp * 256, 256)
-    shocks_here(3)
-    for n in range(HALF):
         relayed(group(10, n), y2, rising[n])
         relayed(group(11, n), y2, falling[n])
 
-    last = quarter(y2)
-    left = jnp.concatenate([er[j, :, last] for j in range(NX)], axis=0)
-    for w in range(4):
-        wide = pl.ds(w * 256, 256)
-        acc[:, wide] = acc[:, wide] + jnp.dot(left, mb[last, wide], preferred_element_type=f32)
-        for k in (2 * w, 2 * w + 1):
-            cols = pl.ds(k * LANES, LANES)
-            log_keep = lpv[:, cols]
-            keep = jnp.broadcast_to(jnp.exp(log_keep), (8, LANES))
-            double = 2.0 * log_keep
-            vol = jnp.broadcast_to(jnp.sqrt(-expm1(double)), (8, LANES))
-            carried = jnp.zeros((8, LANES), f32)
-            for j in range(NX):
-                state = None
-                for i in range(8):
-                    r = pl.ds(j * DAYS + i * 8, 8)
-                    shock = vol * acc[r, cols]
-                    state = shock if i == 0 else (keep * rb[r, :]) * state + shock
-                    acc[r, cols] = state
-                for n, shift in enumerate((1, 2, 4)):
-                    state = state + dk[n, j, :, cols] * pltpu.roll(state, shift, 0)
-                first = jnp.where(sub >= 1, pltpu.roll(state, 1, 0), 0.0)
-                uu[j, :, cols] = first + dx[j, :, cols] * carried
-                carried = dt[j, :, cols] * carried + jnp.broadcast_to(state[7:8], (8, LANES))
-            ebs[k : k + 1, :] = carried[0:1]
+    far = shocks_of(y2)
+    for yy, half in ((ym, falling), (yp, rising)):
+        near = shocks_of(yy)
+        for w in range(2):
+            cols = block(half, w)
+            acc[:, cols] = (
+                acc[:, cols]
+                + jnp.dot(near, mb[quarter(yy), cols], preferred_element_type=f32)
+                + jnp.dot(far, mb[quarter(y2), cols], preferred_element_type=f32)
+            )
+            for k in (half[2 * w], half[2 * w + 1]):
+                cols = columns(k)
+                log_keep = lpv[:, cols]
+                keep = jnp.broadcast_to(jnp.exp(log_keep), (8, LANES))
+                double = 2.0 * log_keep
+                vol = jnp.broadcast_to(jnp.sqrt(-expm1(double)), (8, LANES))
+                carried = jnp.zeros((8, LANES), f32)
+                for j in range(NX):
+                    state = None
+                    for i in range(8):
+                        r = pl.ds(j * DAYS + i * 8, 8)
+                        shock = vol * acc[r, cols]
+                        state = shock if i == 0 else (keep * rb[r, :]) * state + shock
+                        acc[r, cols] = state
+                    for n, shift in enumerate((1, 2, 4)):
+                        state = state + dk[n, j, :, cols] * pltpu.roll(state, shift, 0)
+                    first = jnp.where(sub >= 1, pltpu.roll(state, 1, 0), 0.0)
+                    uu[j, :, cols] = first + dx[j, :, cols] * carried
+                    carried = dt[j, :, cols] * carried + jnp.broadcast_to(state[7:8], (8, LANES))
+                ebs[pl.ds(k, 1), :] = carried[0:1]
 
     for k in FAR_FIRST:
         later(k, lambda k: eb_copy(k).start())
@@ -319,6 +324,11 @@
                 decay = dd[r, cols]
                 acc[r, cols] = acc[r, cols] + decay * u
                 dd[r, cols] = decay * v
+
+    short = scv[...].astype(f32)
+    for k in range(F // LANES):
+        block = jnp.broadcast_to(short[k : k + 1], (LANES, LANES))
+        bm[pl.ds(k * LANES, LANES), pl.ds(K, LANES)] = block.T.astype(bf16)
 
     span = float(BLOCK) * lpd[...]
 

time: 43 us -> 42.8 us (level)
  no operation moved by 1% of the time
where the time goes in v7:
time: 42.8 us; the launch traced here: 42.7 us
  Pallas kernels  42.1 us (98%)
  local copies, waits for them, and re-layouts  0.58 us (1%)
    pallas_call x1, Pallas kernels, local(): pl.pallas_call(kernel, out_shape=jax.ShapeDtypeStruct((PATHS, K), f32), i...  42.1 us

profile of v7, /device:TPU:1, one launch (start us, length us, event | category | flops | bytes accessed | tf_op | source)
XLA Modules:
  0.0 42.7 jit_solution(14848066432295258733)
XLA Ops:
  0.0 42.1 %scenarios.1 = f32[4,128]{1,0:T(4,128)S(1)} custom-call(bf16[64,4,1024]{2,1,0:T(4,128)(2,1)} %e_in.1, f32[4,1024]{1,0:T(4,128)} %s0_in.1, bf16[128,1024]{1,0:T(8,128)(2,1)} %m_in.1, f32[1,1024]{1,0:T(1,128)} %bitcast.4, f32[8,128]{1,0:T(8,128)} %bitcast.5, f32[1,64]{1,0:T(1,128)} %bitcast.7, bf16[1024,128]{1,0:T(8,128)(2,1)} %pay_in.1, bf16[8,128]{1,0:T(8,128)(2,1)} %bitcast.6), custom_call_target="tpu_custom_call" | custom-call | tf_op jit(solution)/shard_map/scenarios/pallas_call | solution.py:409
  42.1 0.6 %copy.9 = f32[4,128]{1,0:T(4,128)} copy(f32[4,128]{1,0:T(4,128)S(1)} %scenarios.1) | data formatting | bytes 4096

commit v8 on v6

--- a/solution.py
+++ b/solution.py
@@ -181,11 +181,6 @@
     for copy in loads[1:]:
         copy.wait()
 
-    short = scv[...].astype(f32)
-    for k in range(F // LANES):
-        block = jnp.broadcast_to(short[k : k + 1], (LANES, LANES))
-        bm[pl.ds(k * LANES, LANES), pl.ds(K, LANES)] = block.T.astype(bf16)
-
     def r_wait(k):
         xx = lax.rem(x + k, NX)
         remote(rw.at[x], rw.at[xx], rsend.at[k - 1], rrecv.at[xx], x=xx).wait_recv()
@@ -320,6 +315,11 @@
                 acc[r, cols] = acc[r, cols] + decay * u
                 dd[r, cols] = decay * v
 
+    short = scv[...].astype(f32)
+    for k in range(F // LANES):
+        block = jnp.broadcast_to(short[k : k + 1], (LANES, LANES))
+        bm[pl.ds(k * LANES, LANES), pl.ds(K, LANES)] = block.T.astype(bf16)
+
     span = float(BLOCK) * lpd[...]
 
     @pl.loop(0, z)
@@ -366,12 +366,16 @@
     fr[pl.ds(mine, 1)] = fs[...][None]
 
     pl.semaphore_wait(met.at[3], NX - 1)
-    for k in (*FAR_FIRST, 0):
-        for n in (2, 1, 3, 0):
-            if k or n:
-                remote(
-                    fs, fr.at[mine], fsend.at[0], frecv.at[0], z=lax.rem(z + k, NZ), x=lax.rem(x + n, NX)
-                ).start()
+    def sums_to(zz, n):
+        return remote(fs, fr.at[mine], fsend.at[0], frecv.at[0], z=zz, x=lax.rem(x + n, NX))
+
+    for zz in range(NZ):
+        for n in (2, 1, 3):
+            sums_to(zz, n).start()
+
+        @pl.when(zz != z)
+        def _():
+            sums_to(zz, 0).start()
 
     for copy in (*straight, *onward, *r_copies, *e_copies):
         copy.wait_send()

time: 43 us -> 42.6 us (level)
  no operation moved by 1% of the time
where the time goes in v8:
time: 42.6 us; the launch traced here: 42.5 us
  Pallas kernels  41.9 us (98%)
  local copies, waits for them, and re-layouts  0.58 us (1%)
    pallas_call x1, Pallas kernels, local(): pl.pallas_call(kernel, out_shape=jax.ShapeDtypeStruct((PATHS, K), f32), i...  41.9 us

profile of v8, /device:TPU:1, one launch (start us, length us, event | category | flops | bytes accessed | tf_op | source)
XLA Modules:
  0.0 42.5 jit_solution(6789515398610319752)
XLA Ops:
  0.0 41.9 %scenarios.1 = f32[4,128]{1,0:T(4,128)S(1)} custom-call(bf16[64,4,1024]{2,1,0:T(4,128)(2,1)} %e_in.1, f32[4,1024]{1,0:T(4,128)} %s0_in.1, bf16[128,1024]{1,0:T(8,128)(2,1)} %m_in.1, f32[1,1024]{1,0:T(1,128)} %bitcast.4, f32[8,128]{1,0:T(8,128)} %bitcast.5, f32[1,64]{1,0:T(1,128)} %bitcast.7, bf16[1024,128]{1,0:T(8,128)(2,1)} %pay_in.1, bf16[8,128]{1,0:T(8,128)(2,1)} %bitcast.6), custom_call_target="tpu_custom_call" | custom-call | tf_op jit(solution)/shard_map/scenarios/pallas_call | solution.py:403
  41.9 0.6 %copy.9 = f32[4,128]{1,0:T(4,128)} copy(f32[4,128]{1,0:T(4,128)S(1)} %scenarios.1) | data formatting | bytes 4096

commit v9 on v8

--- a/solution.py
+++ b/solution.py
@@ -67,6 +67,8 @@
     def quarter(yy):
         return pl.ds(pl.multiple_of(yy * width, width), width)
 
+    own_rows = mb.at[pl.ds(pl.multiple_of((y * 2 + c) * 128, 128), 128), :]
+    mixer = pltpu.make_async_copy(m_in, own_rows, ld.at[7])
     shocks = [
         pltpu.make_async_copy(e_in.at[:, :, quarter(yy)], ev.at[:, :, quarter(yy)], ld.at[9 + n])
         for n, yy in enumerate(turn)
@@ -78,17 +80,11 @@
         pltpu.make_async_copy(s0_in, s0v, ld.at[4]),
         pltpu.make_async_copy(sc_in, scv, ld.at[5]),
         pltpu.make_async_copy(pay_in, bm.at[:, pl.ds(0, K)], ld.at[6]),
-        pltpu.make_async_copy(m_in, mb.at[pl.ds(pl.multiple_of((y * 2 + c) * 128, 128), 128), :], ld.at[7]),
     ]
-    for copy in (*shocks, *loads):
+    for copy in (mixer, *shocks, *loads):
         copy.start()
 
     pl.semaphore_wait(barrier, len(peers) + 2)
-    along_z(met.at[0], 1)
-
-    for peer in beside:
-        pl.semaphore_signal(met.at[4], inc=1, device_id=peer, device_id_type=MESH_ID)
-
     def group(g, n):
         return g * HALF + n
 
@@ -99,16 +95,18 @@
     rising = [HALF * odd + n for n in range(HALF)]
     falling = [HALF * (1 - odd) + n for n in range(HALF)]
 
-    def own(piece):
-        return m_in.at[pl.ds(pl.multiple_of(piece * PIECE, PIECE), PIECE), :]
-
     straight = []
     for n in range(HALF):
-        straight.append(m_copy(group(0, n), own(rising[n]), shard(y, c, rising[n]), y=yp))
-        straight.append(m_copy(group(1, n), own(falling[n]), shard(y, c, falling[n]), y=ym))
-    straight.append(m_copy(group(12, 0), m_in, mb.at[pl.ds(pl.multiple_of((y * 2 + c) * 128, 128), 128), :], c=mate))
+        straight.append(m_copy(group(0, n), shard(y, c, rising[n]), shard(y, c, rising[n]), y=yp))
+        straight.append(m_copy(group(1, n), shard(y, c, falling[n]), shard(y, c, falling[n]), y=ym))
+    straight.append(m_copy(group(12, 0), own_rows, own_rows, c=mate))
+    mixer.wait()
     for copy in straight:
         copy.start()
+    along_z(met.at[0], 1)
+
+    for peer in beside:
+        pl.semaphore_signal(met.at[4], inc=1, device_id=peer, device_id_type=MESH_ID)
 
     loads[0].wait()
     rw[pl.ds(x, 1)] = jnp.ones((1, 8, LANES), f32)

time: 42.6 us -> 42 us (0.986)
  Pallas kernels: 41.9 us -> 41.2 us
    pallas_call x1, Pallas kernels: 41.9 us -> 41.2 us  [local(): pl.pallas_call(kernel, out_shape=jax.ShapeDtypeStruct((PATHS, K), f32), i...]
where the time goes in v9:
time: 42 us; the launch traced here: 41.8 us
  Pallas kernels  41.2 us (98%)
  local copies, waits for them, and re-layouts  0.58 us (1%)
    pallas_call x1, Pallas kernels, local(): pl.pallas_call(kernel, out_shape=jax.ShapeDtypeStruct((PATHS, K), f32), i...  41.2 us

profile of v9, /device:TPU:1, one launch (start us, length us, event | category | flops | bytes accessed | tf_op | source)
XLA Modules:
  0.0 41.8 jit_solution(7804349252766637055)
XLA Ops:
  0.0 41.2 %scenarios.1 = f32[4,128]{1,0:T(4,128)S(1)} custom-call(bf16[64,4,1024]{2,1,0:T(4,128)(2,1)} %e_in.1, f32[4,1024]{1,0:T(4,128)} %s0_in.1, bf16[128,1024]{1,0:T(8,128)(2,1)} %m_in.1, f32[1,1024]{1,0:T(1,128)} %bitcast.4, f32[8,128]{1,0:T(8,128)} %bitcast.5, f32[1,64]{1,0:T(1,128)} %bitcast.7, bf16[1024,128]{1,0:T(8,128)(2,1)} %pay_in.1, bf16[8,128]{1,0:T(8,128)(2,1)} %bitcast.6), custom_call_target="tpu_custom_call" | custom-call | tf_op jit(solution)/shard_map/scenarios/pallas_call | solution.py:401
  41.2 0.6 %copy.9 = f32[4,128]{1,0:T(4,128)} copy(f32[4,128]{1,0:T(4,128)S(1)} %scenarios.1) | data formatting | bytes 4096

commit v10 on v9

--- a/solution.py
+++ b/solution.py
@@ -154,6 +154,13 @@
                 es.at[xx, :, cols], er.at[xx, :, cols], esend.at[n, k - 1], erecv.at[n, xx], x=xx
             ).wait_recv()
 
+    def half(yy, cc, lower):
+        return mb.at[pl.ds(pl.multiple_of((yy * 2 + cc) * 128 + 64 * lower, 64), 64), :]
+
+    def half_relayed(g, yy, lower):
+        there = half(yy, mate, lower)
+        remote(there, there, msend.at[group(g, 0)], mrecv.at[group(g, 0)], c=mate).wait_recv()
+
     def hop(n, yy, piece):
         remote(shard(yy, c, piece), shard(yy, c, piece), msend.at[n], mrecv.at[n], y=yp).wait_recv()
 
@@ -170,11 +177,13 @@
         hop(group(0, n), ym, rising[n])
         passed_on(group(2, n), ym, rising[n], y=yp)
         passed_on(group(4, n), ym, rising[n], **aside[n % 2])
-        passed_on(group(6, n), ym, rising[n], c=mate)
         hop(group(1, n), yp, falling[n])
         passed_on(group(3, n), yp, falling[n], y=ym)
         passed_on(group(5, n), yp, falling[n], **aside[n % 2])
-        passed_on(group(7, n), yp, falling[n], c=mate)
+    straight_halves = ((6, ym, odd), (7, yp, 1 - odd))
+    for g, yy, lower in straight_halves:
+        onward.append(m_copy(group(g, 0), half(yy, c, lower), half(yy, c, lower), c=mate))
+        onward[-1].start()
 
     for copy in loads[1:]:
         copy.wait()
@@ -256,13 +265,13 @@
     remote(m_in, mb.at[pl.ds(pl.multiple_of((y * 2 + mate) * 128, 128), 128), :], msend.at[group(12, 0)], mrecv.at[group(12, 0)], c=mate).wait_recv()
     shocks_here(0)
     product(y * 256, 256, True)
-    for n in range(HALF):
-        relayed(group(6, n), ym, rising[n])
+    half_relayed(*straight_halves[0])
+    for n in range(HALF):
         relayed(group(8, n), ym, falling[n])
     shocks_here(1)
     product(ym * 256, 256)
-    for n in range(HALF):
-        relayed(group(7, n), yp, falling[n])
+    half_relayed(*straight_halves[1])
+    for n in range(HALF):
         relayed(group(9, n), yp, rising[n])
     shocks_here(2)
     product(yp * 256, 256)

time: 42 us -> 41.9 us (level)
  no operation moved by 1% of the time
where the time goes in v10:
time: 41.9 us; the launch traced here: 41.8 us
  Pallas kernels  41.2 us (98%)
  local copies, waits for them, and re-layouts  0.58 us (1%)
    pallas_call x1, Pallas kernels, local(): pl.pallas_call(kernel, out_shape=jax.ShapeDtypeStruct((PATHS, K), f32), i...  41.2 us

profile of v10, /device:TPU:1, one launch (start us, length us, event | category | flops | bytes accessed | tf_op | source)
XLA Modules:
  0.0 41.8 jit_solution(99003887851999861)
XLA Ops:
  0.0 41.2 %scenarios.1 = f32[4,128]{1,0:T(4,128)S(1)} custom-call(bf16[64,4,1024]{2,1,0:T(4,128)(2,1)} %e_in.1, f32[4,1024]{1,0:T(4,128)} %s0_in.1, bf16[128,1024]{1,0:T(8,128)(2,1)} %m_in.1, f32[1,1024]{1,0:T(1,128)} %bitcast.4, f32[8,128]{1,0:T(8,128)} %bitcast.5, f32[1,64]{1,0:T(1,128)} %bitcast.7, bf16[1024,128]{1,0:T(8,128)(2,1)} %pay_in.1, bf16[8,128]{1,0:T(8,128)(2,1)} %bitcast.6), custom_call_target="tpu_custom_call" | custom-call | tf_op jit(solution)/shard_map/scenarios/pallas_call | solution.py:410
  41.2 0.6 %copy.9 = f32[4,128]{1,0:T(4,128)} copy(f32[4,128]{1,0:T(4,128)S(1)} %scenarios.1) | data formatting | bytes 4096

commit v11 on v10

--- a/solution.py
+++ b/solution.py
@@ -140,7 +140,6 @@
             )
             e_copies[-1].start()
         e_own.append(pltpu.make_async_copy(es.at[x, :, cols], er.at[x, :, cols], ld.at[13 + n]))
-        e_own[-1].start()
 
     pl.semaphore_wait(met.at[1], 2)
     along_z(met.at[2], 4)
@@ -185,6 +184,8 @@
         onward.append(m_copy(group(g, 0), half(yy, c, lower), half(yy, c, lower), c=mate))
         onward[-1].start()
 
+    for copy in e_own:
+        copy.start()
     for copy in loads[1:]:
         copy.wait()
 

time: 41.9 us -> 41.9 us (level)
  no operation moved by 1% of the time
where the time goes in v11:
time: 41.9 us; the launch traced here: 41.8 us
  Pallas kernels  41.2 us (98%)
  local copies, waits for them, and re-layouts  0.58 us (1%)
    pallas_call x1, Pallas kernels, local(): pl.pallas_call(kernel, out_shape=jax.ShapeDtypeStruct((PATHS, K), f32), i...  41.2 us

profile of v11, /device:TPU:1, one launch (start us, length us, event | category | flops | bytes accessed | tf_op | source)
XLA Modules:
  0.0 41.8 jit_solution(17576837693454145648)
XLA Ops:
  0.0 41.2 %scenarios.1 = f32[4,128]{1,0:T(4,128)S(1)} custom-call(bf16[64,4,1024]{2,1,0:T(4,128)(2,1)} %e_in.1, f32[4,1024]{1,0:T(4,128)} %s0_in.1, bf16[128,1024]{1,0:T(8,128)(2,1)} %m_in.1, f32[1,1024]{1,0:T(1,128)} %bitcast.4, f32[8,128]{1,0:T(8,128)} %bitcast.5, f32[1,64]{1,0:T(1,128)} %bitcast.7, bf16[1024,128]{1,0:T(8,128)(2,1)} %pay_in.1, bf16[8,128]{1,0:T(8,128)(2,1)} %bitcast.6), custom_call_target="tpu_custom_call" | custom-call | tf_op jit(solution)/shard_map/scenarios/pallas_call | solution.py:411
  41.2 0.6 %copy.9 = f32[4,128]{1,0:T(4,128)} copy(f32[4,128]{1,0:T(4,128)S(1)} %scenarios.1) | data formatting | bytes 4096
